TPU v7x, 32 devices: a whole 2x2x4 slice. The times are simulated.
32 devices in a mesh: vrow: 4 (over z), img: 8 (over y, x, core).
Axes of the slice: x: 2, y: 2, z: 4, core: 2. Of those that a mesh axis runs over, the one named last changes fastest.
Arguments:
- features: bfloat16 [4, 16, 64, 512], P('vrow', None, 'img'), may hold values from -6 to 6
- weight_h: bfloat16 [64, 64, 3, 3], replicated, may hold values from -0.25 to 0.25
- weight_v: bfloat16 [64, 64, 3, 3], replicated, may hold values from -0.25 to 0.25
- beta_h: float32 [5, 64], replicated, may hold values from 0.2 to 1
- beta_v: float32 [5, 64], replicated, may hold values from 0.2 to 1
- shear_set: int32 [5], replicated, may hold values from -2 to 2
- cotangent: bfloat16 [8, 64, 4096], P('vrow', 'img'), may hold values from -6 to 6
Outputs:
- output: bfloat16 [8, 64, 4096], P('vrow', 'img')
- grad_features: bfloat16 [4, 16, 64, 512], P('vrow', None, 'img')
- grad_weight_h: float32 [64, 64, 3, 3], replicated
- grad_weight_v: float32 [64, 64, 3, 3], replicated
- grad_beta_h: float32 [5, 64], replicated
- grad_beta_v: float32 [5, 64], replicated
All inputs are finite; a program needn't handle non-finite values.
Results may differ from a plain program's by a relative error of at most 0.0057.
Values may be sent and summed in bfloat16 or wider, within the bound.
A program may use at most 128 MiB of HBM per device.

v0:
```python
import functools

import jax
import jax.numpy as jnp
from jax import lax
from jax.experimental import pallas as pl
from jax.experimental.pallas import tpu as pltpu
from jax.sharding import PartitionSpec as P

SHIFTS = (-2, -1, 0, 1, 2)
REACH = 3
TAPS = tuple((i, j) for i in (-1, 0, 1) for j in (-1, 0, 1))
LANES = 128
MESH = pl.DeviceIdType.MESH
VMEM_LIMIT = 60 * 1024 * 1024


def place_of(x, shift, shape, start):
    views = lax.broadcasted_iota(jnp.int32, shape, 0) - shape[0] // 2
    return start + x - shift * views


def tap_products(f_ref, w_ref, z_ref):
    _, nxe, nv2, s, _ = z_ref.shape
    nv = nv2 - 2
    zero = jnp.zeros((9, nxe, 1, s, LANES), jnp.float32)
    z_ref[:, :, 0:1] = zero
    z_ref[:, :, nv + 1 : nv + 2] = zero
    source = f_ref[...].reshape(nxe * nv * s, LANES)
    for t in range(0, 9, 2):
        last = min(t + 2, 9)
        got = jnp.dot(
            source, w_ref[:, t * LANES : last * LANES], preferred_element_type=jnp.float32
        )
        for k in range(t, last):
            part = got[:, (k - t) * LANES : (k - t + 1) * LANES]
            z_ref[k, :, 1 : nv + 1] = part.reshape(nxe, nv, s, LANES)


def preact_at(z_ref, x, index, shift, place, total):
    nv = z_ref.shape[2] - 2
    sums = {}
    for t, (i, j) in enumerate(TAPS):
        term = z_ref[t, x + (REACH + j + shift * i), 1 + i : 1 + i + nv]
        sums[j] = term if j not in sums else sums[j] + term
    low = jnp.where(place != 0, sums[-1], 0.0)
    high = jnp.where(place != total - 1, sums[1], 0.0)
    return sums[0] + low + high


def sigma_of(p):
    return 0.5 * jnp.tanh(0.5 * p) + 0.5


def store_dpre(d_ref, r_ref, x, index, place, total, keep, grad, blend, p, sigma):
    nv = grad.shape[0]
    act = jnp.where(keep, p * sigma, 0.0)
    r_ref[index] += jnp.sum(grad * act, axis=0)
    slope = sigma * (1.0 + p * (1.0 - sigma))
    dpre = jnp.where(keep, blend * grad * slope, 0.0)
    d_ref[0, index, x, 1 : nv + 1] = jnp.where(place != 0, dpre, 0.0)
    d_ref[1, index, x, 1 : nv + 1] = dpre
    d_ref[2, index, x, 1 : nv + 1] = jnp.where(place != total - 1, dpre, 0.0)


def clear_dpre(d_ref, r_ref, nx, pad):
    _, count, _, nv2, s, _ = d_ref.shape
    r_ref[...] = jnp.zeros_like(r_ref)
    for j in range(3):
        rim = jnp.zeros((count, pad, nv2, s, LANES), jnp.float32)
        d_ref[j, :, 0:pad] = rim
        d_ref[j, :, pad + nx : 2 * pad + nx] = rim
        side = jnp.zeros((count, nx, 1, s, LANES), jnp.float32)
        d_ref[j, :, pad : pad + nx, 0:1] = side
        d_ref[j, :, pad : pad + nx, nv2 - 1 : nv2] = side


def gather_dpre(d_ref, s_ref):
    nv2, s = d_ref.shape[3:5]
    nv = nv2 - 2

    def body(x, carry):
        for t, (i, j) in enumerate(TAPS):
            total = None
            for index, shift in enumerate(SHIFTS):
                term = d_ref[j + 1, index, x + (REACH - j - shift * i), 1 - i : 1 - i + nv]
                total = term if total is None else total + term
            s_ref[x, :, t * LANES : (t + 1) * LANES] = total.reshape(nv * s, LANES).astype(
                jnp.bfloat16
            )
        return carry

    lax.fori_loop(0, s_ref.shape[0], body, 0)


def pack_grads(source, stacked, r_ref, out_ref):
    wide = lax.dot_general(
        source, stacked, (((0,), (0,)), ((), ())), preferred_element_type=jnp.float32
    )
    half = LANES // 2
    first, second = wide[:half], wide[half:]
    left = lax.broadcasted_iota(jnp.int32, (half, LANES), 1) < half
    sums = jnp.sum(r_ref[...], axis=1)
    sums = sums + pltpu.roll(sums, half, 1)
    for m in range(5):
        low = slice(2 * m * LANES, (2 * m + 1) * LANES)
        even = first[:, low] + pltpu.roll(second[:, low], half, 1)
        if m < 4:
            high = slice((2 * m + 1) * LANES, (2 * m + 2) * LANES)
            odd = pltpu.roll(first[:, high], half, 1) + second[:, high]
        else:
            odd = jnp.concatenate(
                [sums, jnp.zeros((half - sums.shape[0], LANES), jnp.float32)], axis=0
            )
        out_ref[m] = jnp.where(left, even, odd)


def forward_kernel(total, start_ref, f_ref, w_ref, b_ref, h_ref, pre_ref, z_ref):
    nx, nvs, _ = h_ref.shape
    nv, s = pre_ref.shape[2:4]
    start = start_ref[0]
    tap_products(f_ref, w_ref, z_ref)

    def body(x, carry):
        out = f_ref[x + REACH].astype(jnp.float32).reshape(nv, s, LANES)
        for index, shift in enumerate(SHIFTS):
            place = place_of(x, shift, (nv, s, LANES), start)
            p = preact_at(z_ref, x, index, shift, place, total)
            pre_ref[index, x] = p
            keep = (place >= 0) & (place < total)
            out = out + b_ref[index : index + 1] * jnp.where(keep, p * sigma_of(p), 0.0)
        h_ref[x] = out.reshape(nvs, LANES).astype(jnp.bfloat16)
        return carry

    lax.fori_loop(0, nx, body, 0)


def both_kernel(
    nv, total, f_ref, w_ref, b_ref, g_ref, o_ref, e_ref, p_ref, z_ref, d_ref, r_ref, s_ref
):
    nx, nvs, _ = o_ref.shape
    s = nvs // nv
    tap_products(f_ref, w_ref, z_ref)
    clear_dpre(d_ref, r_ref, nx, REACH)

    def body(x, carry):
        out = f_ref[x + REACH].astype(jnp.float32).reshape(nv, s, LANES)
        grad = g_ref[x].astype(jnp.float32).reshape(nv, s, LANES)
        for index, shift in enumerate(SHIFTS):
            place = place_of(x, shift, (nv, s, LANES), 0)
            p = preact_at(z_ref, x, index, shift, place, total)
            sigma = sigma_of(p)
            keep = (place >= 0) & (place < total)
            blend = b_ref[index : index + 1]
            out = out + blend * jnp.where(keep, p * sigma, 0.0)
            store_dpre(
                d_ref, r_ref, x + REACH, index, place, total, keep, grad, blend, p, sigma
            )
        o_ref[x] = out.reshape(nvs, LANES).astype(jnp.bfloat16)
        return carry

    lax.fori_loop(0, nx, body, 0)
    gather_dpre(d_ref, s_ref)
    stacked = s_ref[...].reshape(nx * nvs, 9 * LANES)
    back = lax.dot_general(
        stacked, w_ref[...], (((1,), (1,)), ((), ())), preferred_element_type=jnp.float32
    )
    e_ref[...] = (g_ref[...].astype(jnp.float32) + back.reshape(nx, nvs, LANES)).astype(
        jnp.bfloat16
    )
    source = f_ref[REACH : REACH + nx].reshape(nx * nvs, LANES)
    pack_grads(source, stacked, r_ref, p_ref)


def backward_kernel(
    total,
    start_ref,
    f_ref,
    w_ref,
    b_ref,
    g_ref,
    pre_ref,
    e_ref,
    before_ref,
    after_ref,
    p_ref,
    d_ref,
    r_ref,
    s_ref,
):
    nx, nvs, _ = e_ref.shape
    nv, s = pre_ref.shape[2:4]
    start = start_ref[0]
    clear_dpre(d_ref, r_ref, nx, 2 * REACH)

    def body(x, carry):
        grad = g_ref[x].astype(jnp.float32).reshape(nv, s, LANES)
        for index, shift in enumerate(SHIFTS):
            place = place_of(x, shift, (nv, s, LANES), start)
            p = pre_ref[index, x]
            keep = (place >= 0) & (place < total)
            blend = b_ref[index : index + 1]
            store_dpre(
                d_ref,
                r_ref,
                x + 2 * REACH,
                index,
                place,
                total,
                keep,
                grad,
                blend,
                p,
                sigma_of(p),
            )
        return carry

    lax.fori_loop(0, nx, body, 0)
    gather_dpre(d_ref, s_ref)
    stacked = s_ref[...].reshape((nx + 2 * REACH) * nvs, 9 * LANES)
    back = lax.dot_general(
        stacked, w_ref[...], (((1,), (1,)), ((), ())), preferred_element_type=jnp.float32
    ).reshape(nx + 2 * REACH, nvs, LANES)
    before_ref[...] = back[:REACH].astype(jnp.bfloat16)
    after_ref[...] = back[nx + REACH :].astype(jnp.bfloat16)
    e_ref[...] = g_ref[...].astype(jnp.float32) + back[REACH : REACH + nx]
    source = f_ref[...].reshape((nx + 2 * REACH) * nvs, LANES)
    pack_grads(source, stacked, r_ref, p_ref)


def sum_kernel(
    rows, cols, x_ref, o_ref, part, heard, totals, send_a, recv_a, send_b, recv_b, send_c, recv_c
):
    row, col = lax.axis_index("vrow"), lax.axis_index("img")

    def at(r, c):
        return dict(device_id=(r, c), device_id_type=MESH)

    barrier = pltpu.get_barrier_semaphore()
    for k in range(1, cols):
        pl.semaphore_signal(barrier, inc=1, **at(row, lax.rem(col + k, cols)))
    for k in range(1, rows):
        pl.semaphore_signal(barrier, inc=1, **at(lax.rem(row + k, rows), col))
    pl.semaphore_wait(barrier, cols + rows - 2)

    sends = []
    for k in range(1, cols):
        to = lax.rem(col + k, cols)
        copy = pltpu.make_async_remote_copy(
            src_ref=x_ref.at[to],
            dst_ref=heard.at[k - 1],
            send_sem=send_a.at[k - 1],
            recv_sem=recv_a.at[k - 1],
            **at(row, to),
        )
        copy.start()
        sends.append(copy)
    total = x_ref[col]
    for k, copy in enumerate(sends):
        copy.wait_recv()
        total = total + heard[k]
    part[...] = total
    totals[row] = total
    more = []
    for k in range(1, rows):
        copy = pltpu.make_async_remote_copy(
            src_ref=part,
            dst_ref=totals.at[row],
            send_sem=send_b.at[k - 1],
            recv_sem=recv_b.at[k - 1],
            **at(lax.rem(row + k, rows), col),
        )
        copy.start()
        more.append(copy)
    for copy in more:
        copy.wait_recv()
    total = totals[0]
    for k in range(1, rows):
        total = total + totals[k]
    o_ref[col] = total
    last = []
    for k in range(1, cols):
        copy = pltpu.make_async_remote_copy(
            src_ref=o_ref.at[col],
            dst_ref=o_ref.at[col],
            send_sem=send_c.at[k - 1],
            recv_sem=recv_c.at[k - 1],
            **at(row, lax.rem(col + k, cols)),
        )
        copy.start()
        last.append(copy)
    for copy in last:
        copy.wait_recv()
    for copy in sends + more + last:
        copy.wait_send()


def sum_over_devices(x, rows, cols):
    count, depth, _ = x.shape
    shape = x.shape
    x = x.reshape(cols, count * depth // cols, LANES)
    chunk = x.shape[1:]
    dma = pltpu.SemaphoreType.DMA
    out = pl.pallas_call(
        functools.partial(sum_kernel, rows, cols),
        out_shape=jax.ShapeDtypeStruct(x.shape, jnp.float32),
        in_specs=[pl.BlockSpec(memory_space=pltpu.VMEM)],
        out_specs=pl.BlockSpec(memory_space=pltpu.VMEM),
        scratch_shapes=[
            pltpu.VMEM(chunk, jnp.float32),
            pltpu.VMEM((cols - 1,) + chunk, jnp.float32),
            pltpu.VMEM((rows,) + chunk, jnp.float32),
            dma((cols - 1,)),
            dma((cols - 1,)),
            dma((rows - 1,)),
            dma((rows - 1,)),
            dma((cols - 1,)),
            dma((cols - 1,)),
        ],
        compiler_params=pltpu.CompilerParams(
            collective_id=0, has_side_effects=True, vmem_limit_bytes=VMEM_LIMIT
        ),
        name="sum_over_devices",
    )(x)
    return out.reshape(shape)


def call(kernel, name, args, outs, scratch):
    whole = pl.BlockSpec(memory_space=pltpu.VMEM)
    specs = [
        pl.BlockSpec(memory_space=pltpu.SMEM) if arg.dtype == jnp.int32 else whole for arg in args
    ]
    return pl.pallas_call(
        kernel,
        out_shape=[jax.ShapeDtypeStruct(shape, dtype) for shape, dtype in outs],
        in_specs=specs,
        out_specs=[whole] * len(outs),
        scratch_shapes=[pltpu.VMEM(shape, dtype) for shape, dtype in scratch],
        compiler_params=pltpu.CompilerParams(vmem_limit_bytes=VMEM_LIMIT),
        name=name,
    )(*args)


def halo(leading, trailing, axis):
    count = lax.axis_size(axis)
    up = [(i, i + 1) for i in range(count - 1)]
    down = [(j, i) for i, j in up]
    return lax.ppermute(trailing, axis, up), lax.ppermute(leading, axis, down)


def per_device(features, weight_h, weight_v, beta_h, beta_v, shear_set, cotangent):
    rows, cols = lax.axis_size("vrow"), lax.axis_size("img")
    channels = weight_h.shape[0]
    u_local, y_all, x_local, merged = features.shape
    v_all = merged // channels
    v_local = v_all // rows
    u_all = u_local * rows
    x_all = x_local * cols
    s_h = u_local * y_all // 2
    s_v = v_local * x_local // 2
    f32, bf16 = jnp.float32, jnp.bfloat16
    count = len(SHIFTS)

    weights = jnp.stack([weight_h, weight_v]).reshape(2, channels, channels, 9)
    weights = jnp.transpose(weights, (0, 2, 3, 1))
    eye = jnp.eye(2, dtype=bf16)
    weights = weights[:, None, :, :, None, :] * eye[None, :, None, None, :, None]
    weights = weights.reshape(2, LANES, 9 * LANES)
    chosen = (jnp.asarray(SHIFTS, jnp.int32)[:, None] == shear_set[None, :]).astype(f32)
    betas = jnp.stack([beta_h, beta_v])
    blends = jnp.sum(chosen[None, :, :, None] * betas[:, None], axis=2)
    blends = jnp.tile(blends, (1, 1, 2))

    field = features.reshape(2, s_h, x_local, v_all, channels)
    field = jnp.transpose(field, (2, 3, 1, 0, 4)).reshape(x_local, v_all * s_h, LANES)
    before, after = halo(field[:REACH], field[x_local - REACH :], "img")
    wide = jnp.concatenate([before, field, after], axis=0)
    start = (lax.axis_index("img") * x_local).astype(jnp.int32).reshape(1)
    flat_h = (x_local, v_all * s_h, LANES)
    four_h = (v_all, s_h, LANES)
    hfeat, pre = call(
        functools.partial(forward_kernel, x_all),
        "forward_h",
        [start, wide, weights[0], blends[0]],
        [(flat_h, bf16), ((count, x_local) + four_h, f32)],
        [((9, x_local + 2 * REACH, v_all + 2) + four_h[1:], f32)],
    )

    block = hfeat.reshape(x_local, rows, v_local, s_h, 2, channels)
    block = jnp.transpose(block, (1, 4, 3, 2, 0, 5))
    block = block.reshape(rows, u_local, y_all, v_local * x_local * channels)
    moved = lax.all_to_all(block, "vrow", split_axis=0, concat_axis=0, tiled=True)
    vert = moved.reshape(u_all, y_all, 2, s_v, channels)
    flat_v = (y_all, u_all * s_v, LANES)
    vert = jnp.transpose(vert, (1, 0, 3, 2, 4)).reshape(flat_v)
    vert = jnp.pad(vert, ((REACH, REACH), (0, 0), (0, 0)))
    grad_v = cotangent.reshape(2, s_v, u_all, y_all, channels)
    grad_v = jnp.transpose(grad_v, (3, 2, 1, 0, 4)).reshape(flat_v)
    vout, dvert, packed_v = call(
        functools.partial(both_kernel, u_all, y_all),
        "both_v",
        [vert, weights[1], blends[1], grad_v],
        [(flat_v, bf16), (flat_v, bf16), ((5, channels, LANES), f32)],
        [
            ((9, y_all + 2 * REACH, u_all + 2, s_v, LANES), f32),
            ((3, count, y_all + 2 * REACH, u_all + 2, s_v, LANES), f32),
            ((count, s_v, LANES), f32),
            ((y_all, u_all * s_v, 9 * LANES), bf16),
        ],
    )
    output = jnp.transpose(vout.reshape(y_all, u_all, s_v, 2, channels), (3, 2, 1, 0, 4))
    output = output.reshape(v_local, x_local, u_all * y_all * channels)

    back = jnp.transpose(dvert.reshape(y_all, u_all, s_v, 2, channels), (1, 0, 3, 2, 4))
    back = back.reshape(rows, u_local, y_all, v_local * x_local * channels)
    returned = lax.all_to_all(back, "vrow", split_axis=0, concat_axis=0, tiled=True)
    returned = returned.reshape(rows, 2, s_h, v_local, x_local, channels)
    grad_h = jnp.transpose(returned, (4, 0, 3, 2, 1, 5)).reshape(flat_h)

    rim = (REACH, v_all * s_h, LANES)
    middle, to_before, to_after, packed_h = call(
        functools.partial(backward_kernel, x_all),
        "backward_h",
        [start, wide, weights[0], blends[0], grad_h, pre],
        [(flat_h, f32), (rim, bf16), (rim, bf16), ((5, channels, LANES), f32)],
        [
            ((3, count, x_local + 4 * REACH, v_all + 2) + four_h[1:], f32),
            ((count,) + four_h[1:], f32),
            ((x_local + 2 * REACH, v_all * s_h, 9 * LANES), bf16),
        ],
    )
    from_before, from_after = halo(to_before, to_after, "img")
    gap = ((0, x_local - REACH), (0, 0), (0, 0))
    middle = middle + jnp.pad(from_before, gap).astype(f32)
    middle = middle + jnp.pad(from_after, (gap[0][::-1], (0, 0), (0, 0))).astype(f32)
    dhor = middle.astype(bf16).reshape(x_local, v_all, s_h, 2, channels)
    dhor = jnp.transpose(dhor, (3, 2, 0, 1, 4)).reshape(features.shape)

    packed = jnp.concatenate([packed_h, packed_v], axis=0)
    summed = sum_over_devices(packed, rows, cols).reshape(2, 5, channels, 2, channels)
    factor = float(u_all * v_all * y_all * x_all) ** (-0.5)
    summed = summed * factor
    raw_beta = summed[:, 4, :count, 1]
    by_tap = jnp.transpose(summed, (0, 4, 2, 1, 3)).reshape(2, channels, channels, 10)
    by_tap = by_tap[..., :9].reshape(2, channels, channels, 3, 3)
    grad_beta = jnp.sum(chosen[None, :, :, None] * raw_beta[:, :, None], axis=1)
    return output, dhor, by_tap[0], by_tap[1], grad_beta[0], grad_beta[1]


def solution(mesh):
    placed = (P("vrow", None, "img", None), P(), P(), P(), P(), P(), P("vrow", "img", None))
    return jax.shard_map(
        per_device,
        mesh=mesh,
        in_specs=placed,
        out_specs=(P("vrow", "img", None), P("vrow", None, "img", None), P(), P(), P(), P()),
        check_vma=False,
    )
```

profile of v0, /device:TPU:1, one launch (start us, length us, event | category | flops | bytes accessed | tf_op | source)
XLA Modules:
  0.0 88.9 jit_solution(17230094720593673649)
XLA Ops:
  0.7 1.2 %reshape.143 = bf16[2,8,8,8,64]{4,3,2,1,0:T(8,128)(2,1)S(1)} reshape(bf16[1,16,8,512]{3,2,1,0:T(8,128)(2,1)} %param.8) | data formatting | bytes 262144 | tf_op jit(solution)/shard_map/reshape | solution.py:374
  2.4 4.5 %collective-permute-start = (bf16[3,64,128]{2,1,0:T(8,128)(2,1)S(1)}, bf16[3,64,128]{2,1,0:T(8,128)(2,1)S(1)}, u32[]{:S(2)}, u32[]{:S(2)}) collective-permute-start(bf16[3,64,128]{2,1,0:T(8,128)(2,1)S(1)} %slice.58), channel_id=1, source_target_pairs={{0,1},{1,2},{2,3},{3,4},{4,5},{5,6},{6,7},{8,9},{9,10},{10,11},{11... | collective-permute-start | bytes 147464 | tf_op jit(solution)/shard_map/ppermute | solution.py:348
  7.0 1.9 %collective-permute-start.1 = (bf16[3,64,128]{2,1,0:T(8,128)(2,1)S(1)}, bf16[3,64,128]{2,1,0:T(8,128)(2,1)S(1)}, u32[]{:S(2)}, u32[]{:S(2)}) collective-permute-start(bf16[3,64,128]{2,1,0:T(8,128)(2,1)S(1)} %slice.60), channel_id=1, source_target_pairs={{1,0},{2,1},{3,2},{4,3},{5,4},{6,5},{7,6},{9,8},{10,9},{11,10},{12... | collective-permute-start | bytes 147464 | tf_op jit(solution)/shard_map/ppermute | solution.py:348
  9.8 1.1 %broadcast_multiply_fusion = bf16[2,2,64,9,2,64]{5,4,3,2,1,0:T(2,128)(2,1)S(1)} fusion(bf16[2,2]{1,0:T(2,128)(2,1)S(1)} %compare_convert_fusion.1, bf16[2,64,9,64]{3,2,1,0:T(8,128)(2,1)S(1)} %copy.46), kind=kLoop, calls=%fused_computation | loop fusion | flops 294912 | bytes 737288 | tf_op jit(solution)/shard_map/mul | solution.py:367
  10.8 0.8 fusion
  12.5 1.1 %squeeze.22.w_ref = bf16[128,1152]{1,0:T(8,128)(2,1)} reshape(bf16[1,2,64,9,2,64]{5,4,3,2,1,0:T(2,128)(2,1)S(1)} %get-tuple-element.25) | data formatting | bytes 589824 | tf_op jit(solution)/shard_map/squeeze | solution.py:384
  13.7 0.7 copy-done
  14.4 3.8 %forward_h.1 = (bf16[8,64,128]{2,1,0:T(8,128)(2,1)}, f32[5,8,8,8,128]{4,3,2,1,0:T(8,128)}) custom-call(s32[1]{0:T(128)} %bitcast.start_ref, bf16[14,64,128]{2,1,0:T(8,128)(2,1)} %copy-done, bf16[128,1152]{1,0:T(8,128)(2,1)} %squeeze.22.w_ref, f32[5,128]{1,0:T(8,128)} %tile.14.b_ref), custom_call_target="tpu_custom_call" | custom-call | tf_op jit(solution)/shard_map/forward_h/pallas_call | solution.py:333
  18.1 1.0 %reshape.145 = bf16[8,4,2,8,2,64]{5,4,3,2,1,0:T(2,128)(2,1)S(1)} reshape(bf16[8,64,128]{2,1,0:T(8,128)(2,1)} %get-tuple-element.15) | data formatting | bytes 262144 | tf_op jit(solution)/shard_map/reshape | solution.py:389
  19.4 0.9 reshape.146
  20.2 4.6 %all-to-all-start = ((bf16[4,1,16,1024]{3,2,1,0:T(8,128)(2,1)}), bf16[4,1,16,1024]{3,2,1,0:T(8,128)(2,1)S(1)}, u32[]{:S(2)}, u32[]{:S(2)}) async-start(bf16[4,1,16,1024]{3,2,1,0:T(8,128)(2,1)} %bitcast.8), calls=%async_computation | async-start | bytes 262144 | tf_op jit(solution)/shard_map/all_to_all | solution.py:392
  24.8 0.7 tile.16.b_ref
  26.0 0.8 reshape.150.g_ref
  26.8 1.1 %squeeze.23.w_ref = bf16[128,1152]{1,0:T(8,128)(2,1)} reshape(bf16[1,2,64,9,2,64]{5,4,3,2,1,0:T(2,128)(2,1)S(1)} %get-tuple-element.24) | data formatting | bytes 589824 | tf_op jit(solution)/shard_map/squeeze | solution.py:402
  27.9 1.9 %all-to-all-done = bf16[4,1,16,1024]{3,2,1,0:T(8,128)(2,1)S(1)} async-done(((bf16[4,1,16,1024]{3,2,1,0:T(8,128)(2,1)}), bf16[4,1,16,1024]{3,2,1,0:T(8,128)(2,1)S(1)}, u32[]{:S(2)}, u32[]{:S(2)}) %all-to-all-start) | async-done | bytes 131104 | tf_op jit(solution)/shard_map/all_to_all | solution.py:392
  30.4 0.7 pad.12.f_ref
  31.1 5.6 %both_v.1 = (bf16[16,32,128]{2,1,0:T(8,128)(2,1)}, bf16[16,32,128]{2,1,0:T(8,128)(2,1)}, f32[5,64,128]{2,1,0:T(8,128)}) custom-call(bf16[22,32,128]{2,1,0:T(8,128)(2,1)} %pad.12.f_ref, bf16[128,1152]{1,0:T(8,128)(2,1)} %squeeze.23.w_ref, f32[5,128]{1,0:T(8,128)} %tile.16.b_ref, bf16[16,32,128]{2,1,0:T(8,128)(2,1)} %reshape.150.g_ref), custom_call_target="tpu_custom_call" | custom-call | tf_op jit(solution)/shard_map/both_v/pallas_call | solution.py:333
  36.7 1.1 %reshape.153 = bf16[16,4,8,2,64]{4,3,2,1,0:T(2,128)(2,1)S(1)} reshape(bf16[16,32,128]{2,1,0:T(8,128)(2,1)} %get-tuple-element.17) | data formatting | bytes 262144 | tf_op jit(solution)/shard_map/reshape | solution.py:414
  37.9 0.9 reshape.154
  38.7 3.5 %all-to-all-start.1 = ((bf16[4,1,16,1024]{3,2,1,0:T(8,128)(2,1)}), bf16[4,1,16,1024]{3,2,1,0:T(8,128)(2,1)S(1)}, u32[]{:S(2)}, u32[]{:S(2)}) async-start(bf16[4,1,16,1024]{3,2,1,0:T(8,128)(2,1)} %bitcast.13), calls=%async_computation.1 | async-start | bytes 262144 | tf_op jit(solution)/shard_map/all_to_all | solution.py:416
  42.6 0.9 %reshape.152 = bf16[2,8,4096]{2,1,0:T(8,128)(2,1)} reshape(bf16[2,8,4,16,64]{4,3,2,1,0:T(8,128)(2,1)S(1)} %copy.52) | data formatting | bytes 262144 | tf_op jit(solution)/shard_map/reshape | solution.py:412
  43.5 4.0 %all-to-all-done.1 = bf16[4,1,16,1024]{3,2,1,0:T(8,128)(2,1)S(1)} async-done(((bf16[4,1,16,1024]{3,2,1,0:T(8,128)(2,1)}), bf16[4,1,16,1024]{3,2,1,0:T(8,128)(2,1)S(1)}, u32[]{:S(2)}, u32[]{:S(2)}) %all-to-all-start.1) | async-done | bytes 131104 | tf_op jit(solution)/shard_map/all_to_all | solution.py:416
  48.0 0.8 reshape.156.g_ref
  48.8 5.8 %backward_h.1 = (f32[8,64,128]{2,1,0:T(8,128)}, bf16[3,64,128]{2,1,0:T(8,128)(2,1)}, bf16[3,64,128]{2,1,0:T(8,128)(2,1)}, f32[5,64,128]{2,1,0:T(8,128)}) custom-call(s32[1]{0:T(128)} %bitcast.start_ref, bf16[14,64,128]{2,1,0:T(8,128)(2,1)} %copy-done, bf16[128,1152]{1,0:T(8,128)(2,1)} %squeeze.22.w_ref, f32[5,128]{1,0:T(8,128)} %tile.14.b_ref, ...), custom_call_target="tpu_custom_call" | custom-call | tf_op jit(solution)/shard_map/backward_h/pallas_call | solution.py:333
  54.6 1.7 %pad_maximum_fusion = f32[10,64,128]{2,1,0:T(8,128)} fusion(f32[5,64,128]{2,1,0:T(8,128)S(1)} %copy-done.2, f32[5,64,128]{2,1,0:T(8,128)} %get-tuple-element.22), kind=kLoop, calls=%fused_computation.1 | loop fusion | flops 81920 | bytes 655360 | tf_op jit(solution)/shard_map/concatenate | solution.py:439
  56.3 21.3 %sum_over_devices.1 = f32[8,80,128]{2,1,0:T(8,128)} custom-call(f32[8,80,128]{2,1,0:T(8,128)} %bitcast.61), custom_call_target="tpu_custom_call" | custom-call | tf_op jit(solution)/shard_map/sum_over_devices/pallas_call | solution.py:304
  77.6 1.0 %broadcast_multiply_fusion.1 = f32[8,80,128]{2,1,0:T(8,128)S(1)} fusion(f32[8,80,128]{2,1,0:T(8,128)} %sum_over_devices.1), kind=kLoop, calls=%fused_computation.8 | loop fusion | flops 81920 | bytes 655360 | tf_op jit(solution)/shard_map/mul | solution.py:442
  79.4 3.0 %collective-permute-start.2 = (bf16[3,64,128]{2,1,0:T(8,128)(2,1)S(1)}, bf16[3,64,128]{2,1,0:T(8,128)(2,1)S(1)}, u32[]{:S(2)}, u32[]{:S(2)}) collective-permute-start(bf16[3,64,128]{2,1,0:T(8,128)(2,1)S(1)} %copy-done.12), channel_id=1, source_target_pairs={{0,1},{1,2},{2,3},{3,4},{4,5},{5,6},{6,7},{8,9},{9,10},{10,11},{11... | collective-permute-start | bytes 147464 | tf_op jit(solution)/shard_map/ppermute | solution.py:348
  82.4 1.9 %collective-permute-start.3 = (bf16[3,64,128]{2,1,0:T(8,128)(2,1)S(1)}, bf16[3,64,128]{2,1,0:T(8,128)(2,1)S(1)}, u32[]{:S(2)}, u32[]{:S(2)}) collective-permute-start(bf16[3,64,128]{2,1,0:T(8,128)(2,1)S(1)} %copy-done.11), channel_id=1, source_target_pairs={{1,0},{2,1},{3,2},{4,3},{5,4},{6,5},{7,6},{9,8},{10,9},{11,10},{12... | collective-permute-start | bytes 147464 | tf_op jit(solution)/shard_map/ppermute | solution.py:348
  84.3 0.8 fusion.1
  86.5 1.3 %collective-permute-done.3 = bf16[3,64,128]{2,1,0:T(8,128)(2,1)S(1)} collective-permute-done((bf16[3,64,128]{2,1,0:T(8,128)(2,1)S(1)}, bf16[3,64,128]{2,1,0:T(8,128)(2,1)S(1)}, u32[]{:S(2)}, u32[]{:S(2)}) %collective-permute-start.3) | collective-permute-done | bytes 49184 | tf_op jit(solution)/shard_map/ppermute | solution.py:348
  88.1 0.9 reshape.158
  (70 shorter events, 6.6 us)
Async XLA Ops:
  0.6 8.4 %copy-start.10 = (s32[5]{0:T(128)S(1)}, s32[5]{0:T(128)}, u32[]{:S(2)}) copy-start(s32[5]{0:T(128)} %constant.15.clone) | copy-start | bytes 64
  0.6 8.3 %copy-start.7 = (f32[5,64]{1,0:T(8,128)S(1)}, f32[5,64]{1,0:T(8,128)}, u32[]{:S(2)}) copy-start(f32[5,64]{1,0:T(8,128)} %param.12) | copy-start | bytes 3844
  0.7 8.3 %copy-start.8 = (f32[5,64]{1,0:T(8,128)S(1)}, f32[5,64]{1,0:T(8,128)}, u32[]{:S(2)}) copy-start(f32[5,64]{1,0:T(8,128)} %param.11) | copy-start | bytes 3844
  0.7 8.4 %copy-start.9 = (s32[5]{0:T(128)S(1)}, s32[5]{0:T(128)}, u32[]{:S(2)}) copy-start(s32[5]{0:T(128)} %param.13) | copy-start | bytes 64
  0.7 8.6 %copy-start.3 = (bf16[64,64,3,3]{1,0,3,2:T(8,128)(2,1)S(1)}, bf16[64,64,3,3]{1,0,3,2:T(8,128)(2,1)}, u32[]{:S(2)}) copy-start(bf16[64,64,3,3]{1,0,3,2:T(8,128)(2,1)} %param.10) | copy-start | bytes 221188
  0.7 8.6 %copy-start.4 = (bf16[64,64,3,3]{1,0,3,2:T(8,128)(2,1)S(1)}, bf16[64,64,3,3]{1,0,3,2:T(8,128)(2,1)}, u32[]{:S(2)}) copy-start(bf16[64,64,3,3]{1,0,3,2:T(8,128)(2,1)} %param.9) | copy-start | bytes 221188
  2.4 11.2 %collective-permute-start = (bf16[3,64,128]{2,1,0:T(8,128)(2,1)S(1)}, bf16[3,64,128]{2,1,0:T(8,128)(2,1)S(1)}, u32[]{:S(2)}, u32[]{:S(2)}) collective-permute-start(bf16[3,64,128]{2,1,0:T(8,128)(2,1)S(1)} %slice.58), channel_id=1, source_target_pairs={{0,1},{1,2},{2,3},{3,4},{4,5},{5,6},{6,7},{8,9},{9,10},{10,11},{11... | collective-permute-start | bytes 147464 | tf_op jit(solution)/shard_map/ppermute | solution.py:348
  7.0 6.6 %collective-permute-start.1 = (bf16[3,64,128]{2,1,0:T(8,128)(2,1)S(1)}, bf16[3,64,128]{2,1,0:T(8,128)(2,1)S(1)}, u32[]{:S(2)}, u32[]{:S(2)}) collective-permute-start(bf16[3,64,128]{2,1,0:T(8,128)(2,1)S(1)} %slice.60), channel_id=1, source_target_pairs={{1,0},{2,1},{3,2},{4,3},{5,4},{6,5},{7,6},{9,8},{10,9},{11,10},{12... | collective-permute-start | bytes 147464 | tf_op jit(solution)/shard_map/ppermute | solution.py:348
  13.6 11.9 %copy-start.5 = (bf16[2,8,4096]{2,1,0:T(8,128)(2,1)S(1)}, bf16[2,8,4096]{2,1,0:T(8,128)(2,1)}, u32[]{:S(2)}) copy-start(bf16[2,8,4096]{2,1,0:T(8,128)(2,1)} %param.14) | copy-start | bytes 393220
  13.7 0.7 copy-start
  20.2 9.6 %all-to-all-start = ((bf16[4,1,16,1024]{3,2,1,0:T(8,128)(2,1)}), bf16[4,1,16,1024]{3,2,1,0:T(8,128)(2,1)S(1)}, u32[]{:S(2)}, u32[]{:S(2)}) async-start(bf16[4,1,16,1024]{3,2,1,0:T(8,128)(2,1)} %bitcast.8), calls=%async_computation | async-start | bytes 262144 | tf_op jit(solution)/shard_map/all_to_all | solution.py:392
  36.7 5.5 %copy-start.6 = (bf16[16,32,128]{2,1,0:T(8,128)(2,1)S(1)}, bf16[16,32,128]{2,1,0:T(8,128)(2,1)}, u32[]{:S(2)}) copy-start(bf16[16,32,128]{2,1,0:T(8,128)(2,1)} %get-tuple-element.16) | copy-start | bytes 393220
  38.7 8.8 %all-to-all-start.1 = ((bf16[4,1,16,1024]{3,2,1,0:T(8,128)(2,1)}), bf16[4,1,16,1024]{3,2,1,0:T(8,128)(2,1)S(1)}, u32[]{:S(2)}, u32[]{:S(2)}) async-start(bf16[4,1,16,1024]{3,2,1,0:T(8,128)(2,1)} %bitcast.13), calls=%async_computation.1 | async-start | bytes 262144 | tf_op jit(solution)/shard_map/all_to_all | solution.py:416
  48.0 6.6 %copy-start.2 = (f32[5,64,128]{2,1,0:T(8,128)S(1)}, f32[5,64,128]{2,1,0:T(8,128)}, u32[]{:S(2)}) copy-start(f32[5,64,128]{2,1,0:T(8,128)} %get-tuple-element.23) | copy-start | bytes 491524
  78.6 0.8 copy-start.12
  78.6 3.8 %copy-start.11 = (bf16[3,64,128]{2,1,0:T(8,128)(2,1)S(1)}, bf16[3,64,128]{2,1,0:T(8,128)(2,1)}, u32[]{:S(2)}) copy-start(bf16[3,64,128]{2,1,0:T(8,128)(2,1)} %get-tuple-element.21) | copy-start | bytes 147460
  79.0 8.8 %copy-start.1 = (f32[8,64,128]{2,1,0:T(8,128)S(1)}, f32[8,64,128]{2,1,0:T(8,128)}, u32[]{:S(2)}) copy-start(f32[8,64,128]{2,1,0:T(8,128)} %get-tuple-element.19) | copy-start | bytes 786436
  79.4 7.1 %collective-permute-start.2 = (bf16[3,64,128]{2,1,0:T(8,128)(2,1)S(1)}, bf16[3,64,128]{2,1,0:T(8,128)(2,1)S(1)}, u32[]{:S(2)}, u32[]{:S(2)}) collective-permute-start(bf16[3,64,128]{2,1,0:T(8,128)(2,1)S(1)} %copy-done.12), channel_id=1, source_target_pairs={{0,1},{1,2},{2,3},{3,4},{4,5},{5,6},{6,7},{8,9},{9,10},{10,11},{11... | collective-permute-start | bytes 147464 | tf_op jit(solution)/shard_map/ppermute | solution.py:348
  82.4 5.4 %collective-permute-start.3 = (bf16[3,64,128]{2,1,0:T(8,128)(2,1)S(1)}, bf16[3,64,128]{2,1,0:T(8,128)(2,1)S(1)}, u32[]{:S(2)}, u32[]{:S(2)}) collective-permute-start(bf16[3,64,128]{2,1,0:T(8,128)(2,1)S(1)} %copy-done.11), channel_id=1, source_target_pairs={{1,0},{2,1},{3,2},{4,3},{5,4},{6,5},{7,6},{9,8},{10,9},{11,10},{12... | collective-permute-start | bytes 147464 | tf_op jit(solution)/shard_map/ppermute | solution.py:348
where the time goes:
time: 89.6 us; the launch traced here: 88.9 us
  Pallas kernels  36.5 us (41%)
  local copies, waits for them, and re-layouts  20.5 us (23%)
  starting transfers between devices  19.4 us (22%)
  waiting for transfers between devices  7.27 us (8%)
  other arithmetic  4.12 us (5%)
  between operations  1.15 us (1%)
    pallas_call x1, Pallas kernels, sum_over_devices(): pl.pallas_call(functools.partial(sum_kernel, rows, cols), out_shape=jax.S...  21.3 us
    pallas_call x3, Pallas kernels, call(): pl.pallas_call(kernel, out_shape=[jax.ShapeDtypeStruct(shape, dtype) for...  15.2 us
    ppermute x4, starting transfers between devices, halo(): return (lax.ppermute(trailing, axis, up), lax.ppermute(leading, axis, down))  11.3 us
    all_to_all x1, starting transfers between devices, per_device(): lax.all_to_all(block, 'vrow', split_axis=0, concat_axis=0, tiled=True)  4.59 us
    all_to_all x1, waiting for transfers between devices, per_device(): lax.all_to_all(back, 'vrow', split_axis=0, concat_axis=0, tiled=True)  4.01 us
    all_to_all x1, starting transfers between devices, per_device(): lax.all_to_all(back, 'vrow', split_axis=0, concat_axis=0, tiled=True)  3.51 us
    unnamed x32, local copies, waits for them, and re-layouts  1.96 us
    all_to_all x1, waiting for transfers between devices, per_device(): lax.all_to_all(block, 'vrow', split_axis=0, concat_axis=0, tiled=True)  1.93 us
  transfers between devices with their start and end apart: 6, of which 3 were waited for; matrix products, arithmetic and copies ran while one was open for 12% of the time, Pallas kernels for 0%

commit v1 on v0

v1 whole, which is shorter than its diff:
```python
import functools

import jax
import jax.numpy as jnp
from jax import lax
from jax.experimental import pallas as pl
from jax.experimental.pallas import tpu as pltpu
from jax.sharding import PartitionSpec as P

SHIFTS = (-2, -1, 0, 1, 2)
REACH = 3
TAPS = tuple((i, j) for i in (-1, 0, 1) for j in (-1, 0, 1))
LANES = 128
MESH = pl.DeviceIdType.MESH
VMEM_LIMIT = 60 * 1024 * 1024


def place_of(x, shift, shape, start):
    views = lax.broadcasted_iota(jnp.int32, shape, 0) - shape[0] // 2
    return start + x - shift * views


def tap_products(f_ref, w_ref, which, z_ref, first, length):
    _, _, nv2, s, _ = z_ref.shape
    nv = nv2 - 2
    source = f_ref[first : first + length].reshape(length * nv * s, LANES)
    for t in range(0, 9, 2):
        last = min(t + 2, 9)
        got = jnp.dot(
            source, w_ref[which, :, t * LANES : last * LANES], preferred_element_type=jnp.float32
        )
        for k in range(t, last):
            part = got[:, (k - t) * LANES : (k - t + 1) * LANES]
            z_ref[k, first : first + length, 1 : nv + 1] = part.reshape(length, nv, s, LANES)


def clear_products(z_ref):
    _, nxe, nv2, s, _ = z_ref.shape
    zero = jnp.zeros((9, nxe, 1, s, LANES), jnp.float32)
    z_ref[:, :, 0:1] = zero
    z_ref[:, :, nv2 - 1 : nv2] = zero


def preact_at(z_ref, x, index, shift, place, total):
    nv = z_ref.shape[2] - 2
    sums = {}
    for t, (i, j) in enumerate(TAPS):
        term = z_ref[t, x + (REACH + j + shift * i), 1 + i : 1 + i + nv]
        sums[j] = term if j not in sums else sums[j] + term
    low = jnp.where(place != 0, sums[-1], 0.0)
    high = jnp.where(place != total - 1, sums[1], 0.0)
    return sums[0] + low + high


def sigma_of(p):
    return 0.5 * jnp.tanh(0.5 * p) + 0.5


def store_dpre(d_ref, r_ref, x, index, place, total, keep, grad, blend, p, sigma):
    nv = grad.shape[0]
    act = jnp.where(keep, p * sigma, 0.0)
    r_ref[index] += jnp.sum(grad * act, axis=0)
    slope = sigma * (1.0 + p * (1.0 - sigma))
    dpre = jnp.where(keep, blend * grad * slope, 0.0)
    d_ref[0, index, x, 1 : nv + 1] = jnp.where(place != 0, dpre, 0.0)
    d_ref[1, index, x, 1 : nv + 1] = dpre
    d_ref[2, index, x, 1 : nv + 1] = jnp.where(place != total - 1, dpre, 0.0)


def clear_dpre(d_ref, r_ref, nx, pad):
    _, count, _, nv2, s, _ = d_ref.shape
    r_ref[...] = jnp.zeros_like(r_ref)
    for j in range(3):
        rim = jnp.zeros((count, pad, nv2, s, LANES), jnp.float32)
        d_ref[j, :, 0:pad] = rim
        d_ref[j, :, pad + nx : 2 * pad + nx] = rim
        side = jnp.zeros((count, nx, 1, s, LANES), jnp.float32)
        d_ref[j, :, pad : pad + nx, 0:1] = side
        d_ref[j, :, pad : pad + nx, nv2 - 1 : nv2] = side


def gather_dpre(d_ref, s_ref, length):
    nv2, s = d_ref.shape[3:5]
    nv = nv2 - 2

    def body(x, carry):
        for t, (i, j) in enumerate(TAPS):
            total = None
            for index, shift in enumerate(SHIFTS):
                term = d_ref[j + 1, index, x + (REACH - j - shift * i), 1 - i : 1 - i + nv]
                total = term if total is None else total + term
            here = pl.ds(pl.multiple_of(x * (nv * s), 16), nv * s)
            s_ref[here, t * LANES : (t + 1) * LANES] = total.reshape(nv * s, LANES).astype(
                jnp.bfloat16
            )
        return carry

    lax.fori_loop(0, length, body, 0)


def pack_grads(source, stacked, r_ref, out_ref, which):
    wide = lax.dot_general(
        source, stacked, (((0,), (0,)), ((), ())), preferred_element_type=jnp.float32
    )
    half = LANES // 2
    first, second = wide[:half], wide[half:]
    left = lax.broadcasted_iota(jnp.int32, (half, LANES), 1) < half
    sums = jnp.sum(r_ref[...], axis=1)
    sums = sums + pltpu.roll(sums, half, 1)
    for m in range(5):
        low = slice(2 * m * LANES, (2 * m + 1) * LANES)
        even = first[:, low] + pltpu.roll(second[:, low], half, 1)
        if m < 4:
            high = slice((2 * m + 1) * LANES, (2 * m + 2) * LANES)
            odd = pltpu.roll(first[:, high], half, 1) + second[:, high]
        else:
            odd = jnp.concatenate(
                [sums, jnp.zeros((half - sums.shape[0], LANES), jnp.float32)], axis=0
            )
        out_ref[which, m * half : (m + 1) * half] = jnp.where(left, even, odd)


def half_roll(x):
    return pltpu.roll(x, LANES // 2, x.ndim - 1)


def remote(src, dst, sems, k, device):
    return pltpu.make_async_remote_copy(
        src_ref=src,
        dst_ref=dst,
        send_sem=sems.at[0, k],
        recv_sem=sems.at[1, k],
        device_id=device,
        device_id_type=MESH,
    )


class Sum:
    def __init__(self, rows, cols, x_ref, o_ref, heard, totals, sem_a, sem_b, sem_c):
        self.rows, self.cols = rows, cols
        self.x_ref, self.o_ref, self.heard, self.totals = x_ref, o_ref, heard, totals
        self.sems = (sem_a, sem_b, sem_c)
        self.row, self.col = lax.axis_index("vrow"), lax.axis_index("img")
        self.size = heard.shape[1]
        self.sent = []

    def chunk(self, index):
        return pl.ds(pl.multiple_of(index * self.size, 8), self.size)

    def scatter(self):
        self.first = []
        for k in range(1, self.cols):
            to = lax.rem(self.col + k, self.cols)
            source = self.x_ref.at[self.chunk(to)]
            copy = remote(source, self.heard.at[k - 1], self.sems[0], k - 1, (self.row, to))
            copy.start()
            self.first.append(copy)

    def exchange(self):
        total = self.x_ref[self.chunk(self.col)]
        for k, copy in enumerate(self.first):
            copy.wait_recv()
            total = total + self.heard[k]
        self.totals[self.row] = total
        self.second = []
        for k in range(1, self.rows):
            to = lax.rem(self.row + k, self.rows)
            mine = self.totals.at[self.row]
            copy = remote(mine, mine, self.sems[1], k - 1, (to, self.col))
            copy.start()
            self.second.append(copy)

    def gather(self):
        for copy in self.second:
            copy.wait_recv()
        total = self.totals[0]
        for k in range(1, self.rows):
            total = total + self.totals[k]
        self.o_ref[self.chunk(self.col)] = total
        self.third = []
        for k in range(1, self.cols):
            to = lax.rem(self.col + k, self.cols)
            mine = self.o_ref.at[self.chunk(self.col)]
            copy = remote(mine, mine, self.sems[2], k - 1, (self.row, to))
            copy.start()
            self.third.append(copy)

    def finish(self):
        for copy in self.third:
            copy.wait_recv()
        for copy in self.first + self.second + self.third:
            copy.wait_send()


def field_kernel(
    rows,
    cols,
    f_ref,
    c_ref,
    w_ref,
    b_ref,
    o_ref,
    dhor_ref,
    sum_ref,
    wide,
    pre_ref,
    hfeat,
    send_h,
    got_h,
    vert,
    dvert,
    send_v,
    got_v,
    grad_h,
    rim_sent,
    rim_got,
    payload,
    heard,
    totals,
    s_ref,
    r_h,
    r_v,
    halo_sem,
    there_sem,
    back_sem,
    rim_sem,
    sum_a,
    sum_b,
    sum_c,
):
    row, col = lax.axis_index("vrow"), lax.axis_index("img")
    _, nx, nv, s, _ = pre_ref.shape
    ny, nu, sv, _ = dvert.shape
    x_all = nx * cols
    start = col * nx
    count = len(SHIFTS)
    f32, bf16 = jnp.float32, jnp.bfloat16
    left = lax.broadcasted_iota(jnp.int32, (1, 1, LANES), 2) < LANES // 2
    right_col, left_col = lax.rem(col + 1, cols), lax.rem(col + cols - 1, cols)

    barrier = pltpu.get_barrier_semaphore()
    for k in range(1, cols):
        peer = (row, lax.rem(col + k, cols))
        pl.semaphore_signal(barrier, inc=1, device_id=peer, device_id_type=MESH)
    for k in range(1, rows):
        peer = (lax.rem(row + k, rows), col)
        pl.semaphore_signal(barrier, inc=1, device_id=peer, device_id_type=MESH)
    pl.semaphore_wait(barrier, cols + rows - 2)

    halo = [
        remote(
            f_ref.at[pl.ds(nx - REACH, REACH)],
            wide.at[pl.ds(0, REACH)],
            halo_sem,
            0,
            (row, right_col),
        ),
        remote(
            f_ref.at[pl.ds(0, REACH)],
            wide.at[pl.ds(nx + REACH, REACH)],
            halo_sem,
            1,
            (row, left_col),
        ),
    ]
    for copy in halo:
        copy.start()

    for copy in halo:
        copy.wait_recv()

    @pl.when(col == 0)
    def _():
        wide[:REACH] = jnp.zeros((REACH,) + wide.shape[1:], bf16)

    @pl.when(col == cols - 1)
    def _():
        wide[nx + REACH :] = jnp.zeros((REACH,) + wide.shape[1:], bf16)

    wide[REACH : REACH + nx] = f_ref[...]
    there = []

    def first_pass(z_ref):
        clear_products(z_ref)
        tap_products(wide, w_ref, 0, z_ref, 0, nx + 2 * REACH)

        def body(x, carry):
            out = f_ref[x].astype(f32).reshape(nv, s, LANES)
            for index, shift in enumerate(SHIFTS):
                place = place_of(x, shift, (nv, s, LANES), start)
                p = preact_at(z_ref, x, index, shift, place, x_all)
                pre_ref[index, x] = p
                keep = (place >= 0) & (place < x_all)
                out = out + b_ref[0, index : index + 1] * jnp.where(keep, p * sigma_of(p), 0.0)
            hfeat[x] = out
            return carry

        lax.fori_loop(0, nx, body, 0)

    pl.run_scoped(first_pass, pltpu.VMEM((9, nx + 2 * REACH, nv + 2, s, LANES), f32))

    def block_there(to):
        views = hfeat[:, pl.ds(2 * to, 2)]
        one, two = views[:, 0], views[:, 1]
        low = jnp.swapaxes(jnp.where(left, one, half_roll(two)), 0, 1)
        high = jnp.swapaxes(jnp.where(left, half_roll(one), two), 0, 1)
        return jnp.concatenate([low, high], axis=0).reshape(ny * sv, LANES).astype(bf16)

    for k in range(1, rows):
        to = lax.rem(row + k, rows)
        send_h[k - 1] = block_there(to)
        copy = remote(send_h.at[k - 1], got_h.at[row], there_sem, k - 1, (to, col))
        copy.start()
        there.append(copy)
    got_h[row] = block_there(row)

    sum_v = Sum(
        rows,
        cols,
        payload.at[1],
        sum_ref.at[1],
        heard.at[1],
        totals.at[1],
        sum_a.at[1],
        sum_b.at[1],
        sum_c.at[1],
    )
    sum_h = Sum(
        rows,
        cols,
        payload.at[0],
        sum_ref.at[0],
        heard.at[0],
        totals.at[0],
        sum_a.at[0],
        sum_b.at[0],
        sum_c.at[0],
    )
    back = []

    for copy in there:
        copy.wait_recv()
    parts = [got_h[u].astype(f32).reshape(ny, 1, sv, LANES) for u in range(rows)]
    vert[REACH : REACH + ny] = (
        jnp.concatenate(parts, axis=1).reshape(ny, nu * sv, LANES).astype(bf16)
    )

    def second_pass(z_ref, d_ref):
        clear_products(z_ref)
        clear_dpre(d_ref, r_v, ny, REACH)
        vert[:REACH] = jnp.zeros((REACH,) + vert.shape[1:], bf16)
        vert[ny + REACH :] = jnp.zeros((REACH,) + vert.shape[1:], bf16)
        rim = jnp.zeros((9, REACH, nu, sv, LANES), f32)
        z_ref[:, :REACH, 1 : nu + 1] = rim
        z_ref[:, ny + REACH :, 1 : nu + 1] = rim
        tap_products(vert, w_ref, 1, z_ref, REACH, ny)

        def body(y, carry):
            out = vert[y + REACH].astype(f32).reshape(nu, sv, LANES)
            grad = c_ref[y].astype(f32).reshape(nu, sv, LANES)
            for index, shift in enumerate(SHIFTS):
                place = place_of(y, shift, (nu, sv, LANES), 0)
                p = preact_at(z_ref, y, index, shift, place, ny)
                sigma = sigma_of(p)
                keep = (place >= 0) & (place < ny)
                blend = b_ref[1, index : index + 1]
                out = out + blend * jnp.where(keep, p * sigma, 0.0)
                store_dpre(
                    d_ref, r_v, y + REACH, index, place, ny, keep, grad, blend, p, sigma
                )
            o_ref[y] = out.reshape(nu * sv, LANES).astype(bf16)
            return carry

        lax.fori_loop(0, ny, body, 0)
        gather_dpre(d_ref, s_ref, ny)

    pl.run_scoped(
        second_pass,
        pltpu.VMEM((9, ny + 2 * REACH, nu + 2, sv, LANES), f32),
        pltpu.VMEM((3, count, ny + 2 * REACH, nu + 2, sv, LANES), f32),
    )
    stacked = s_ref[: ny * nu * sv]
    grads = lax.dot_general(
        stacked, w_ref[1], (((1,), (1,)), ((), ())), preferred_element_type=f32
    )
    dvert[...] = c_ref[...].astype(f32).reshape(dvert.shape) + grads.reshape(dvert.shape)

    def block_back(to):
        block = dvert[:, pl.ds(to, 1)].reshape(ny, sv, LANES)
        low = jnp.swapaxes(block[:s], 0, 1)
        high = jnp.swapaxes(block[s:], 0, 1)
        one = jnp.where(left, low, half_roll(high))
        two = jnp.where(left, half_roll(low), high)
        both = jnp.concatenate([one[:, None], two[:, None]], axis=1)
        return both.reshape(nx, 2 * s, LANES).astype(bf16)

    for k in range(1, rows):
        to = lax.rem(row + k, rows)
        send_v[k - 1] = block_back(to)
        copy = remote(send_v.at[k - 1], got_v.at[row], back_sem, k - 1, (to, col))
        copy.start()
        back.append(copy)
    got_v[row] = block_back(row)
    source = vert[REACH : REACH + ny].reshape(ny * nu * sv, LANES)
    pack_grads(source, stacked, r_v, payload, 1)
    sum_v.scatter()


    for copy in back:
        copy.wait_recv()
    for r in range(rows):
        grad_h[:, r * 2 * s : (r + 1) * 2 * s] = got_v[r].astype(f32)

    def third_pass(d_ref):
        clear_dpre(d_ref, r_h, nx, 2 * REACH)
        def body(x, carry):
            grad = grad_h[x].reshape(nv, s, LANES)
            for index, shift in enumerate(SHIFTS):
                place = place_of(x, shift, (nv, s, LANES), start)
                p = pre_ref[index, x]
                keep = (place >= 0) & (place < x_all)
                blend = b_ref[0, index : index + 1]
                sigma = sigma_of(p)
                store_dpre(
                    d_ref,
                    r_h,
                    x + 2 * REACH,
                    index,
                    place,
                    x_all,
                    keep,
                    grad,
                    blend,
                    p,
                    sigma,
                )
            return carry

        lax.fori_loop(0, nx, body, 0)
        gather_dpre(d_ref, s_ref, nx + 2 * REACH)

    pl.run_scoped(
        third_pass,
        pltpu.VMEM((3, count, nx + 4 * REACH, nv + 2, s, LANES), f32),
    )
    sum_v.exchange()
    stacked = s_ref[: (nx + 2 * REACH) * nv * s]
    source = wide[...].reshape((nx + 2 * REACH) * nv * s, LANES)
    pack_grads(source, stacked, r_h, payload, 0)
    sum_h.scatter()
    sum_v.gather()
    grads = lax.dot_general(
        stacked, w_ref[0], (((1,), (1,)), ((), ())), preferred_element_type=f32
    ).reshape(nx + 2 * REACH, nv * s, LANES)
    rim_sent[0] = grads[:REACH].astype(bf16)
    rim_sent[1] = grads[nx + REACH :].astype(bf16)
    grad_h[...] += grads[REACH : REACH + nx]

    rims = [
        remote(rim_sent.at[0], rim_got.at[1], rim_sem, 0, (row, left_col)),
        remote(rim_sent.at[1], rim_got.at[0], rim_sem, 1, (row, right_col)),
    ]
    for copy in rims:
        copy.start()
    sum_h.exchange()
    for copy in rims:
        copy.wait_recv()

    @pl.when(col > 0)
    def _():
        grad_h[:REACH] += rim_got[0].astype(f32)

    @pl.when(col < cols - 1)
    def _():
        grad_h[nx - REACH :] += rim_got[1].astype(f32)

    dhor_ref[...] = grad_h[...].astype(bf16)
    sum_h.gather()
    for copy in halo + there + back + rims:
        copy.wait_send()
    sum_v.finish()
    sum_h.finish()


def per_device(features, weight_h, weight_v, beta_h, beta_v, shear_set, cotangent):
    rows, cols = lax.axis_size("vrow"), lax.axis_size("img")
    channels = weight_h.shape[0]
    u_local, y_all, x_local, merged = features.shape
    v_all = merged // channels
    v_local = v_all // rows
    u_all = u_local * rows
    x_all = x_local * cols
    s_h = u_local * y_all // 2
    s_v = v_local * x_local // 2
    f32, bf16 = jnp.float32, jnp.bfloat16
    count = len(SHIFTS)
    assert u_local == 1 and v_local == 2

    weights = jnp.stack([weight_h, weight_v]).reshape(2, channels, channels, 9)
    weights = jnp.transpose(weights, (0, 2, 3, 1))
    eye = jnp.eye(2, dtype=bf16)
    weights = weights[:, None, :, :, None, :] * eye[None, :, None, None, :, None]
    weights = weights.reshape(2, LANES, 9 * LANES)
    chosen = (jnp.asarray(SHIFTS, jnp.int32)[:, None] == shear_set[None, :]).astype(f32)
    betas = jnp.stack([beta_h, beta_v])
    blends = jnp.sum(chosen[None, :, :, None] * betas[:, None], axis=2)
    blends = jnp.tile(blends, (1, 1, 2))

    field = features.reshape(2, s_h, x_local, v_all, channels)
    field = jnp.transpose(field, (2, 3, 1, 0, 4)).reshape(x_local, v_all * s_h, LANES)
    grad_v = cotangent.reshape(2, s_v, u_all, y_all, channels)
    grad_v = jnp.transpose(grad_v, (3, 2, 1, 0, 4)).reshape(y_all, u_all * s_v, LANES)
    flat_h = (x_local, v_all * s_h, LANES)
    flat_v = (y_all, u_all * s_v, LANES)
    rim = (REACH, v_all * s_h, LANES)
    grads = 5 * channels
    chunk = (grads // cols, LANES)
    vmem, dma = pltpu.VMEM, pltpu.SemaphoreType.DMA
    whole = pl.BlockSpec(memory_space=vmem)
    vout, dhor, summed = pl.pallas_call(
        functools.partial(field_kernel, rows, cols),
        out_shape=[
            jax.ShapeDtypeStruct(flat_v, bf16),
            jax.ShapeDtypeStruct(flat_h, bf16),
            jax.ShapeDtypeStruct((2, grads, LANES), f32),
        ],
        in_specs=[whole] * 4,
        out_specs=[whole] * 3,
        scratch_shapes=[
            vmem((x_local + 2 * REACH,) + flat_h[1:], bf16),
            vmem((count, x_local, v_all, s_h, LANES), f32),
            vmem((x_local, v_all, s_h, LANES), f32),
            vmem((rows - 1, y_all * s_v, LANES), bf16),
            vmem((rows, y_all * s_v, LANES), bf16),
            vmem((y_all + 2 * REACH,) + flat_v[1:], bf16),
            vmem((y_all, u_all, s_v, LANES), f32),
            vmem((rows - 1, x_local, 2 * s_h, LANES), bf16),
            vmem((rows, x_local, 2 * s_h, LANES), bf16),
            vmem(flat_h, f32),
            vmem((2,) + rim, bf16),
            vmem((2,) + rim, bf16),
            vmem((2, grads, LANES), f32),
            vmem((2, cols - 1) + chunk, f32),
            vmem((2, rows) + chunk, f32),
            vmem((max((x_local + 2 * REACH) * flat_h[1], y_all * flat_v[1]), 9 * LANES), bf16),
            vmem((count, s_h, LANES), f32),
            vmem((count, s_v, LANES), f32),
            dma((2, 2)),
            dma((2, rows - 1)),
            dma((2, rows - 1)),
            dma((2, 2)),
            dma((2, 2, cols - 1)),
            dma((2, 2, rows - 1)),
            dma((2, 2, cols - 1)),
        ],
        compiler_params=pltpu.CompilerParams(
            collective_id=0, has_side_effects=True, vmem_limit_bytes=VMEM_LIMIT
        ),
        name="light_field",
    )(field, grad_v, weights, blends)
    output = jnp.transpose(vout.reshape(y_all, u_all, s_v, 2, channels), (3, 2, 1, 0, 4))
    output = output.reshape(v_local, x_local, u_all * y_all * channels)
    dhor = dhor.reshape(x_local, v_all, s_h, 2, channels)
    dhor = jnp.transpose(dhor, (3, 2, 0, 1, 4)).reshape(features.shape)
    summed = summed.reshape(2, 5, channels, 2, channels)
    factor = float(u_all * v_all * y_all * x_all) ** (-0.5)
    summed = summed * factor
    raw_beta = summed[:, 4, :count, 1]
    by_tap = jnp.transpose(summed, (0, 4, 2, 1, 3)).reshape(2, channels, channels, 10)
    by_tap = by_tap[..., :9].reshape(2, channels, channels, 3, 3)
    grad_beta = jnp.sum(chosen[None, :, :, None] * raw_beta[:, :, None], axis=1)
    return output, dhor, by_tap[0], by_tap[1], grad_beta[0], grad_beta[1]


def solution(mesh):
    placed = (P("vrow", None, "img", None), P(), P(), P(), P(), P(), P("vrow", "img", None))
    return jax.shard_map(
        per_device,
        mesh=mesh,
        in_specs=placed,
        out_specs=(P("vrow", "img", None), P("vrow", None, "img", None), P(), P(), P(), P()),
        check_vma=False,
    )
```

time: 89.6 us -> 56.8 us (0.63)
  starting transfers between devices: 19.4 us -> 0 us
  local copies, waits for them, and re-layouts: 20.5 us -> 10.3 us
  waiting for transfers between devices: 7.27 us -> 0 us
  Pallas kernels: 36.5 us -> 40.5 us
    ppermute x4 -> x0, starting transfers between devices: 11.3 us -> none  [halo(): return (lax.ppermute(trailing, axis, up), lax.ppermute(leading, axis, down))]
    all_to_all x2 -> x0, starting transfers between devices: 8.1 us -> none  [the longest x1 4.59 us: per_device(): lax.all_to_all(block, 'vrow', split_axis=0, concat_axis=0, tiled=True)]
    all_to_all x2 -> x0, waiting for transfers between devices: 5.95 us -> none  [the longest x1 4.01 us: per_device(): lax.all_to_all(back, 'vrow', split_axis=0, concat_axis=0, tiled=True)]
    reshape x12 -> x2, local copies, waits for them, and re-layouts: 6.29 us -> 0.94 us  [the longest x1 0.81 us: per_device(): jnp.transpose(grad_v, (3, 2, 1, 0, 4)).reshape(y_all, u_all * s_v, LANES)]
    pallas_call x4 -> x1, Pallas kernels: 36.5 us -> 40.5 us  [per_device(): pl.pallas_call(functools.partial(field_kernel, rows, cols), out_shape=[ja...]
    squeeze x2 -> x0, local copies, waits for them, and re-layouts: 2.14 us -> none  [the longest x1 1.07 us: per_device(): weights[1]]
    mul x0 -> x4, local copies, waits for them, and re-layouts: none -> 2.04 us  [per_device(): weights[:, None, :, :, None, :] * eye[None, :, None, None, :, None]]
    concatenate x1 -> x0, other arithmetic: 1.67 us -> none  [per_device(): packed = jnp.concatenate([packed_h, packed_v], axis=0)]
  transfers between devices with their start and end apart: 6 -> 0, of which waited for: 3 -> 0; matrix products, arithmetic and copies ran while one was open for 12% -> 0% of each run, Pallas kernels for 0% -> 0%
where the time goes in v1:
time: 56.8 us; the launch traced here: 56.2 us
  Pallas kernels  40.5 us (71%)
  local copies, waits for them, and re-layouts  10.3 us (18%)
  other arithmetic  4.58 us (8%)
  between operations  0.84 us (1%)
    pallas_call x1, Pallas kernels, per_device(): pl.pallas_call(functools.partial(field_kernel, rows, cols), out_shape=[ja...  40.5 us
    mul x4, local copies, waits for them, and re-layouts, per_device(): weights[:, None, :, :, None, :] * eye[None, :, None, None, :, None]  2.04 us

profile of v1, /device:TPU:1, one launch (start us, length us, event | category | flops | bytes accessed | tf_op | source)
XLA Modules:
  0.0 56.2 jit_solution(14264370286035259363)
XLA Ops:
  0.6 0.7 %compare_convert_fusion = f32[5,5]{1,0:T(8,128)S(1)} fusion(s32[5]{0:T(128)} %param.13, s32[5]{0:T(128)} %constant.6.clone), kind=kLoop, calls=%fused_computation.11 | loop fusion | flops 50 | bytes 140 | tf_op jit(solution)/shard_map/convert_element_type | solution.py:504
  1.4 0.7 %pad_maximum_fusion = f32[2,5,64]{2,1,0:T(8,128)S(1)} fusion(f32[1,5,64]{2,1,0:T(8,128)} %bitcast.44, f32[1,5,64]{2,1,0:T(8,128)} %bitcast.45), kind=kLoop, calls=%fused_computation.7 | loop fusion | flops 640 | bytes 5120 | tf_op jit(solution)/shard_map/stack | solution.py:505
  2.1 0.1 multiply_reduce_fusion.1
  2.2 0.1 tile.10
  2.3 0.6 %copy.32.b_ref = f32[2,5,128]{2,1,0:T(8,128)} copy(f32[2,5,128]{2,0,1:T(2,128)S(1)} %tile.10) | data formatting | bytes 10240 | tf_op jit(solution)/shard_map/tile | solution.py:507
  2.9 1.0 %maximum_bitcast_fusion = bf16[2,64,9,64]{1,3,2,0:T(8,128)(2,1)S(1)} fusion(bf16[1,64,64,9]{2,1,3,0:T(8,128)(2,1)} %bitcast.41, bf16[1,64,64,9]{2,1,3,0:T(8,128)(2,1)} %bitcast.42), kind=kLoop, calls=%fused_computation | loop fusion | flops 73728 | bytes 294912 | tf_op jit(solution)/shard_map/transpose | solution.py:500
  3.9 0.4 copy.30
  4.4 0.6 %mul.55 = bf16[2,2,64,9,2,64]{5,4,3,2,1,0:T(2,128)(2,1)S(1)} broadcast(bf16[2,64,9,64]{3,2,1,0:T(8,128)(2,1)S(1)} %copy.30), dimensions={0,2,3,5} | broadcast | bytes 737280 | tf_op jit(solution)/shard_map/mul | solution.py:502
  5.0 0.7 %mul.56 = bf16[2,128,1152]{2,1,0:T(8,128)(2,1)S(1)} reshape(bf16[2,2,64,9,2,64]{5,4,3,2,1,0:T(2,128)(2,1)S(1)} %mul.55) | data formatting | bytes 1179648 | tf_op jit(solution)/shard_map/mul | solution.py:502
  5.7 0.4 mul.57
  6.1 0.0 copy-start
  6.1 0.4 mul.58
  6.5 0.9 %broadcast_multiply_fusion.w_ref = bf16[2,128,1152]{2,1,0:T(8,128)(2,1)} fusion(bf16[2,128,1152]{2,1,0:T(8,128)(2,1)S(1)} %mul.56, bf16[128,1152]{1,0:T(8,128)(2,1)S(1)} %mul.58), kind=kLoop, calls=%fused_computation.1 | loop fusion | flops 294912 | bytes 1474560 | tf_op jit(solution)/shard_map/mul | solution.py:502
  7.4 0.2 reshape.100
  7.6 0.3 copy.46
  7.8 0.8 %reshape.101.f_ref = bf16[8,64,128]{2,1,0:T(8,128)(2,1)} reshape(bf16[8,8,8,2,64]{4,3,2,1,0:T(2,128)(2,1)S(1)} %bitcast.35) | data formatting | bytes 262144 | tf_op jit(solution)/shard_map/reshape | solution.py:510
  8.7 0.2 reshape.102
  8.9 0.3 copy.45
  9.2 0.8 %reshape.103.c_ref = bf16[16,32,128]{2,1,0:T(8,128)(2,1)} reshape(bf16[16,4,8,2,64]{4,3,2,1,0:T(2,128)(2,1)S(1)} %bitcast.36) | data formatting | bytes 262144 | tf_op jit(solution)/shard_map/reshape | solution.py:512
  10.0 40.5 %light_field.1 = (bf16[16,32,128]{2,1,0:T(8,128)(2,1)}, bf16[8,64,128]{2,1,0:T(8,128)(2,1)}, f32[2,320,128]{2,1,0:T(8,128)}) custom-call(bf16[8,64,128]{2,1,0:T(8,128)(2,1)} %reshape.101.f_ref, bf16[16,32,128]{2,1,0:T(8,128)(2,1)} %reshape.103.c_ref, bf16[2,128,1152]{2,1,0:T(8,128)(2,1)} %broadcast_multiply_fusion.w_ref, f32[2,5,128]{2,1,0:T(8,128)} %copy.32.b_ref), custom_call_target="tpu_custom_call" | custom-call | tf_op jit(solution)/shard_map/light_field/pallas_call | solution.py:520
  50.5 1.0 %broadcast_multiply_fusion.1 = f32[2,320,128]{2,1,0:T(8,128)S(1)} fusion(f32[2,320,128]{2,1,0:T(8,128)} %get-tuple-element.11), kind=kLoop, calls=%fused_computation.4 | loop fusion | flops 81920 | bytes 655360 | tf_op jit(solution)/shard_map/mul | solution.py:567
  51.5 0.4 mul.66
  51.9 0.1 multiply_reduce_fusion
  52.0 0.6 %copy_bitcast_fusion.3 = (f32[5,64]{1,0:T(8,128)}, f32[5,64]{1,0:T(8,128)}) fusion(f32[1,5,64]{2,0,1:T(1,128)S(1)} %get-tuple-element.14, f32[1,5,64]{2,0,1:T(1,128)S(1)} %get-tuple-element.15), kind=kLoop, calls=%fused_computation.9 | loop fusion | bytes 5120
  52.6 0.4 copy.35
  53.0 0.8 %fusion = (f32[1,64,64,9]{2,1,3,0:T(8,128)}, f32[1,64,64,9]{2,1,3,0:T(8,128)}) fusion(f32[2,64,64,10]{2,1,3,0:T(8,128)S(1)} %bitcast.34), kind=kLoop, calls=%fused_computation.13 | loop fusion | bytes 589824 | tf_op jit(solution)/shard_map/slice | solution.py:572
  53.9 0.1 reshape.104
  54.0 0.2 copy.33
  54.2 0.9 %reshape.105 = bf16[2,8,4096]{2,1,0:T(8,128)(2,1)} reshape(bf16[2,8,4,16,64]{4,3,2,1,0:T(8,128)(2,1)S(1)} %copy.33) | data formatting | bytes 262144 | tf_op jit(solution)/shard_map/reshape | solution.py:562
  55.2 0.1 reshape.106
  55.3 0.1 copy.34
  55.4 0.9 %reshape.107 = bf16[1,16,8,512]{3,2,1,0:T(8,128)(2,1)} reshape(bf16[2,8,8,8,64]{4,3,2,1,0:T(8,128)(2,1)S(1)} %copy.34) | data formatting | bytes 262144 | tf_op jit(solution)/shard_map/reshape | solution.py:564
  (13 shorter events, 0.1 us)
Async XLA Ops:
  6.1 1.3 %copy-start = (bf16[1,16,8,512]{3,2,1,0:T(8,128)(2,1)S(1)}, bf16[1,16,8,512]{3,2,1,0:T(8,128)(2,1)}, u32[]{:S(2)}) copy-start(bf16[1,16,8,512]{3,2,1,0:T(8,128)(2,1)} %param.8) | copy-start | bytes 393220
  6.5 2.2 %copy-start.1 = (bf16[2,8,4096]{2,1,0:T(8,128)(2,1)S(1)}, bf16[2,8,4096]{2,1,0:T(8,128)(2,1)}, u32[]{:S(2)}) copy-start(bf16[2,8,4096]{2,1,0:T(8,128)(2,1)} %param.14) | copy-start | bytes 393220
  52.6 1.2 %copy-start.3 = (bf16[16,32,128]{2,1,0:T(8,128)(2,1)S(1)}, bf16[16,32,128]{2,1,0:T(8,128)(2,1)}, u32[]{:S(2)}) copy-start(bf16[16,32,128]{2,1,0:T(8,128)(2,1)} %get-tuple-element.9) | copy-start | bytes 393220
  53.0 2.1 %copy-start.2 = (bf16[8,64,128]{2,1,0:T(8,128)(2,1)S(1)}, bf16[8,64,128]{2,1,0:T(8,128)(2,1)}, u32[]{:S(2)}) copy-start(bf16[8,64,128]{2,1,0:T(8,128)(2,1)} %get-tuple-element.10) | copy-start | bytes 393220

commit v2 on v1

v2 whole, which is shorter than its diff:
```python
import functools

import jax
import jax.numpy as jnp
from jax import lax
from jax.experimental import pallas as pl
from jax.experimental.pallas import tpu as pltpu
from jax.sharding import PartitionSpec as P

SHIFTS = (-2, -1, 0, 1, 2)
REACH = 3
TAPS = tuple((i, j) for i in (-1, 0, 1) for j in (-1, 0, 1))
LANES = 128
MESH = pl.DeviceIdType.MESH
VMEM_LIMIT = 60 * 1024 * 1024


def place_of(x, shift, views, shape, start):
    view = lax.broadcasted_iota(jnp.int32, shape, 0) // (shape[0] // views) - views // 2
    return start + x - shift * view


def dot_t(x, y):
    return lax.dot_general(x, y, (((1,), (1,)), ((), ())), preferred_element_type=jnp.float32)


def tap_products(f_ref, w_ref, which, z_ref, views, first, length):
    rows = f_ref.shape[1]
    per = rows // 8
    step = per // views * (views + 2)
    source = f_ref[first : first + length].reshape(length * rows, LANES)
    for t in range(0, 9, 2):
        last = min(t + 2, 9)
        got = dot_t(source, w_ref[which, t * LANES : last * LANES])
        for k in range(t, last):
            part = got[:, (k - t) * LANES : (k - t + 1) * LANES]
            for x in range(length):
                here = (first + x) * step + per // views
                z_ref[k, here : here + per] = part[x * rows : (x + 1) * rows].reshape(
                    per, 8, LANES
                )


def clear_products(z_ref, columns, views, group, rim):
    step = (views + 2) * group
    side = jnp.zeros((9, group, 8, LANES), jnp.float32)

    def body(x, carry):
        z_ref[:, pl.ds(x * step, group)] = side
        z_ref[:, pl.ds(x * step + (views + 1) * group, group)] = side
        return carry

    lax.fori_loop(0, columns, body, 0)
    if rim:
        zero = jnp.zeros((9, rim * step, 8, LANES), jnp.float32)
        z_ref[:, : rim * step] = zero
        z_ref[:, (columns - rim) * step : columns * step] = zero


def preact_at(z_ref, x, views, group, shift, place, total):
    step = (views + 2) * group
    sums = {}
    for t, (i, j) in enumerate(TAPS):
        here = (x + (REACH + j + shift * i)) * step + (1 + i) * group
        term = z_ref[t, pl.ds(here, views * group)]
        sums[j] = term if j not in sums else sums[j] + term
    low = jnp.where(place != 0, sums[-1], 0.0)
    high = jnp.where(place != total - 1, sums[1], 0.0)
    return sums[0] + low + high


def sigma_of(p):
    return 0.5 * jnp.tanh(0.5 * p) + 0.5


def store_dpre(d_ref, r_ref, x, index, group, keep, grad, blend, p, sigma):
    act = jnp.where(keep, p * sigma, 0.0)
    r_ref[index] += jnp.sum(grad * act, axis=0)
    slope = sigma * (1.0 + p * (1.0 - sigma))
    dpre = jnp.where(keep, blend * grad * slope, 0.0)
    d_ref[index, x, group : group + grad.shape[0]] = dpre


def clear_dpre(d_ref, r_ref, nx, pad, group):
    count, _, per, _, _ = d_ref.shape
    r_ref[...] = jnp.zeros_like(r_ref)
    rim = jnp.zeros((count, pad, per, 8, LANES), jnp.float32)
    d_ref[:, 0:pad] = rim
    d_ref[:, pad + nx : 2 * pad + nx] = rim
    side = jnp.zeros((count, nx, group, 8, LANES), jnp.float32)
    d_ref[:, pad : pad + nx, 0:group] = side
    d_ref[:, pad : pad + nx, per - group : per] = side


def gather_dpre(d_ref, s_ref, length, views, group, start, total):
    per = views * group

    def body(x, carry):
        sums = [None] * 9
        for index, shift in enumerate(SHIFTS):
            place = place_of(x, shift, views, (per, 8, LANES), start)
            inside = (place >= 0) & (place < total)
            for t, (i, j) in enumerate(TAPS):
                term = d_ref[
                    index, x + (REACH - j - shift * i), (1 - i) * group : (1 - i) * group + per
                ]
                if j != 0:
                    term = jnp.where(inside, term, 0.0)
                sums[t] = term if sums[t] is None else sums[t] + term
        here = pl.ds(pl.multiple_of(x * (per * 8), 16), per * 8)
        for t in range(9):
            s_ref[here, t * LANES : (t + 1) * LANES] = (
                sums[t].reshape(per * 8, LANES).astype(jnp.bfloat16)
            )
        return carry

    lax.fori_loop(0, length, body, 0)


def pack_grads(source, stacked, r_ref, out_ref, which):
    wide = lax.dot_general(
        source, stacked, (((0,), (0,)), ((), ())), preferred_element_type=jnp.float32
    )
    half = LANES // 2
    first, second = wide[:half], wide[half:]
    left = lax.broadcasted_iota(jnp.int32, (half, LANES), 1) < half
    sums = jnp.sum(r_ref[...], axis=1)
    sums = sums + pltpu.roll(sums, half, 1)
    for m in range(5):
        low = slice(2 * m * LANES, (2 * m + 1) * LANES)
        even = first[:, low] + pltpu.roll(second[:, low], half, 1)
        if m < 4:
            high = slice((2 * m + 1) * LANES, (2 * m + 2) * LANES)
            odd = pltpu.roll(first[:, high], half, 1) + second[:, high]
        else:
            odd = jnp.concatenate(
                [sums, jnp.zeros((half - sums.shape[0], LANES), jnp.float32)], axis=0
            )
        out_ref[which, m * half : (m + 1) * half] = jnp.where(left, even, odd)


def exchange_halves(one, two, left):
    return jnp.where(left, one, half_roll(two)), jnp.where(left, half_roll(one), two)


def stack_weights(weight_ref, w_ref, which, left):
    half = LANES // 2
    for t in range(9):
        tap = weight_ref[t].astype(jnp.float32)
        twice = jnp.concatenate([tap, tap], axis=1)
        both = jnp.concatenate(
            [jnp.where(left, twice, 0.0), jnp.where(left, 0.0, twice)], axis=0
        )
        w_ref[which, t * LANES : (t + 1) * LANES] = both.astype(jnp.bfloat16)


def stack_blends(beta_ref, shear_ref, b_ref, which):
    beta = beta_ref[...]
    beta = jnp.concatenate([beta, beta], axis=1)
    for index, shift in enumerate(SHIFTS):
        total = jnp.zeros((1, LANES), jnp.float32)
        for k in range(beta.shape[0]):
            total = total + jnp.where(shear_ref[k] == shift, 1.0, 0.0) * beta[k : k + 1]
        b_ref[which, index : index + 1] = total


def unpack_grads(sum_ref, which, shear_ref, weight_ref, beta_ref, factor):
    half = LANES // 2
    for m in range(5):
        tile = sum_ref[which, m * half : (m + 1) * half] * factor
        turned = jnp.transpose(tile)
        weight_ref[2 * m] = turned[:half]
        if m < 4:
            weight_ref[2 * m + 1] = turned[half:]
        else:
            raw = half_roll(tile[:8])[:, :half]
    for k in range(beta_ref.shape[0]):
        total = jnp.zeros((1, half), jnp.float32)
        for index, shift in enumerate(SHIFTS):
            total = total + jnp.where(shear_ref[k] == shift, 1.0, 0.0) * raw[index : index + 1]
        beta_ref[k : k + 1] = total


def half_roll(x):
    return pltpu.roll(x, LANES // 2, x.ndim - 1)


def remote(src, dst, sems, k, device):
    return pltpu.make_async_remote_copy(
        src_ref=src,
        dst_ref=dst,
        send_sem=sems.at[0, k],
        recv_sem=sems.at[1, k],
        device_id=device,
        device_id_type=MESH,
    )


class Sum:
    def __init__(self, rows, cols, x_ref, o_ref, heard, totals, sem_a, sem_b, sem_c):
        self.rows, self.cols = rows, cols
        self.x_ref, self.o_ref, self.heard, self.totals = x_ref, o_ref, heard, totals
        self.sems = (sem_a, sem_b, sem_c)
        self.row, self.col = lax.axis_index("vrow"), lax.axis_index("img")
        self.size = heard.shape[1]
        self.sent = []

    def chunk(self, index):
        return pl.ds(pl.multiple_of(index * self.size, 8), self.size)

    def scatter(self):
        self.first = []
        for k in range(1, self.cols):
            to = lax.rem(self.col + k, self.cols)
            source = self.x_ref.at[self.chunk(to)]
            copy = remote(source, self.heard.at[k - 1], self.sems[0], k - 1, (self.row, to))
            copy.start()
            self.first.append(copy)

    def exchange(self):
        total = self.x_ref[self.chunk(self.col)]
        for k, copy in enumerate(self.first):
            copy.wait_recv()
            total = total + self.heard[k]
        self.totals[self.row] = total
        self.second = []
        for k in range(1, self.rows):
            to = lax.rem(self.row + k, self.rows)
            mine = self.totals.at[self.row]
            copy = remote(mine, mine, self.sems[1], k - 1, (to, self.col))
            copy.start()
            self.second.append(copy)

    def gather(self):
        for copy in self.second:
            copy.wait_recv()
        total = self.totals[0]
        for k in range(1, self.rows):
            total = total + self.totals[k]
        self.o_ref[self.chunk(self.col)] = total
        self.third = []
        for k in range(1, self.cols):
            to = lax.rem(self.col + k, self.cols)
            mine = self.o_ref.at[self.chunk(self.col)]
            copy = remote(mine, mine, self.sems[2], k - 1, (self.row, to))
            copy.start()
            self.third.append(copy)

    def finish(self):
        for copy in self.third:
            copy.wait_recv()
        for copy in self.first + self.second + self.third:
            copy.wait_send()


def field_kernel(
    rows,
    cols,
    f_ref,
    weight_h_ref,
    weight_v_ref,
    beta_h_ref,
    beta_v_ref,
    shear_ref,
    c_ref,
    o_ref,
    dhor_ref,
    gw_h_ref,
    gw_v_ref,
    gb_h_ref,
    gb_v_ref,
    wide,
    w_ref,
    b_ref,
    z_ref,
    pre_ref,
    hfeat,
    send_h,
    got_h,
    vert,
    cot,
    vout,
    dvert,
    send_v,
    got_v,
    grad_h,
    rim_sent,
    rim_got,
    payload,
    sum_ref,
    heard,
    totals,
    s_ref,
    d_h,
    d_v,
    r_h,
    r_v,
    halo_sem,
    there_sem,
    back_sem,
    rim_sem,
    sum_a,
    sum_b,
    sum_c,
):
    row, col = lax.axis_index("vrow"), lax.axis_index("img")
    nx, nvs, _ = grad_h.shape
    ny, nu, sv, _ = dvert.shape
    s = f_ref.shape[0] // 2
    nv = nvs // s
    gh, gv = s // 8, sv // 8
    x_all = nx * cols
    start = col * nx
    f32, bf16 = jnp.float32, jnp.bfloat16
    shape_h, shape_v = (nv * gh, 8, LANES), (nu * gv, 8, LANES)
    left = lax.broadcasted_iota(jnp.int32, (1, 1, LANES), 2) < LANES // 2
    left2 = lax.broadcasted_iota(jnp.int32, (1, LANES), 1) < LANES // 2
    right_col, left_col = lax.rem(col + 1, cols), lax.rem(col + cols - 1, cols)

    barrier = pltpu.get_barrier_semaphore()
    for k in range(1, cols):
        peer = (row, lax.rem(col + k, cols))
        pl.semaphore_signal(barrier, inc=1, device_id=peer, device_id_type=MESH)
    for k in range(1, rows):
        peer = (lax.rem(row + k, rows), col)
        pl.semaphore_signal(barrier, inc=1, device_id=peer, device_id_type=MESH)

    for m in range(nv // 2):
        block = f_ref[:, :, m * LANES : (m + 1) * LANES].astype(f32)
        low, high = jnp.swapaxes(block[:s], 0, 1), jnp.swapaxes(block[s:], 0, 1)
        both = jnp.concatenate(exchange_halves(low, high, left), axis=1)
        wide[REACH : REACH + nx, m * 2 * s : (m + 1) * 2 * s] = both.astype(bf16)
    pl.semaphore_wait(barrier, cols + rows - 2)

    halo = [
        remote(
            wide.at[pl.ds(nx, REACH)],
            wide.at[pl.ds(0, REACH)],
            halo_sem,
            0,
            (row, right_col),
        ),
        remote(
            wide.at[pl.ds(REACH, REACH)],
            wide.at[pl.ds(nx + REACH, REACH)],
            halo_sem,
            1,
            (row, left_col),
        ),
    ]
    for copy in halo:
        copy.start()
    stack_weights(weight_h_ref, w_ref, 0, left2)
    stack_blends(beta_h_ref, shear_ref, b_ref, 0)
    clear_products(z_ref, nx + 2 * REACH, nv, gh, 0)
    tap_products(wide, w_ref, 0, z_ref, nv, REACH, nx)
    for copy in halo:
        copy.wait_recv()

    @pl.when(col == 0)
    def _():
        wide[:REACH] = jnp.zeros((REACH, nvs, LANES), bf16)

    @pl.when(col == cols - 1)
    def _():
        wide[nx + REACH :] = jnp.zeros((REACH, nvs, LANES), bf16)

    tap_products(wide, w_ref, 0, z_ref, nv, 0, REACH)
    tap_products(wide, w_ref, 0, z_ref, nv, nx + REACH, REACH)

    def first_pass(x, carry):
        out = wide[x + REACH].astype(f32).reshape(shape_h)
        for index, shift in enumerate(SHIFTS):
            place = place_of(x, shift, nv, shape_h, start)
            p = preact_at(z_ref, x, nv, gh, shift, place, x_all)
            pre_ref[index, x] = p
            keep = (place >= 0) & (place < x_all)
            out = out + b_ref[0, index : index + 1] * jnp.where(keep, p * sigma_of(p), 0.0)
        hfeat[x] = out.reshape(nv, s, LANES)
        return carry

    lax.fori_loop(0, nx, first_pass, 0)

    def block_there(to):
        views = hfeat[:, pl.ds(2 * to, 2)]
        low, high = exchange_halves(views[:, 0], views[:, 1], left)
        both = [jnp.swapaxes(low, 0, 1), jnp.swapaxes(high, 0, 1)]
        return jnp.concatenate(both, axis=0).reshape(ny * sv, LANES).astype(bf16)

    there = []
    for k in range(1, rows):
        to = lax.rem(row + k, rows)
        send_h[k - 1] = block_there(to)
        copy = remote(send_h.at[k - 1], got_h.at[row], there_sem, k - 1, (to, col))
        copy.start()
        there.append(copy)
    got_h[row] = block_there(row)

    sum_h, sum_v = [
        Sum(
            rows,
            cols,
            payload.at[n],
            sum_ref.at[n],
            heard.at[n],
            totals.at[n],
            sum_a.at[n],
            sum_b.at[n],
            sum_c.at[n],
        )
        for n in range(2)
    ]
    stack_weights(weight_v_ref, w_ref, 1, left2)
    stack_blends(beta_v_ref, shear_ref, b_ref, 1)
    clear_products(z_ref, ny + 2 * REACH, nu, gv, REACH)
    clear_dpre(d_v, r_v, ny, REACH, gv)
    for u in range(nu):
        for m in range(ny // 2):
            here = (u * ny // 2 + m) * LANES
            one = c_ref[0, :, here : here + LANES].astype(f32)
            two = c_ref[1, :, here : here + LANES].astype(f32)
            cot[2 * m, u], cot[2 * m + 1, u] = exchange_halves(one, two, left2)
    for copy in there:
        copy.wait_recv()
    parts = [got_h[u].astype(f32).reshape(ny, 1, sv, LANES) for u in range(rows)]
    vert[...] = jnp.concatenate(parts, axis=1).reshape(ny, nu * sv, LANES).astype(bf16)

    for t in range(0, 9, 2):
        last = min(t + 2, 9)
        got = dot_t(vert[...].reshape(ny * nu * sv, LANES), w_ref[1, t * LANES : last * LANES])
        for k in range(t, last):
            part = got[:, (k - t) * LANES : (k - t + 1) * LANES]
            for y in range(ny):
                here = (REACH + y) * (nu + 2) * gv + gv
                z_ref[k, here : here + nu * gv] = part[y * nu * sv : (y + 1) * nu * sv].reshape(
                    shape_v
                )

    def second_pass(y, carry):
        out = vert[y].astype(f32).reshape(shape_v)
        grad = cot[y].reshape(shape_v)
        for index, shift in enumerate(SHIFTS):
            place = place_of(y, shift, nu, shape_v, 0)
            p = preact_at(z_ref, y, nu, gv, shift, place, ny)
            sigma = sigma_of(p)
            keep = (place >= 0) & (place < ny)
            blend = b_ref[1, index : index + 1]
            out = out + blend * jnp.where(keep, p * sigma, 0.0)
            store_dpre(d_v, r_v, y + REACH, index, gv, keep, grad, blend, p, sigma)
        vout[y] = out.reshape(nu, sv, LANES)
        return carry

    lax.fori_loop(0, ny, second_pass, 0)
    gather_dpre(d_v, s_ref, ny, nu, gv, 0, ny)
    stacked = s_ref[: ny * nu * sv]
    grads = jnp.dot(stacked, w_ref[1], preferred_element_type=f32)
    dvert[...] = cot[...] + grads.reshape(dvert.shape)

    def block_back(to):
        block = dvert[:, pl.ds(to, 1)].reshape(ny, sv, LANES)
        low, high = jnp.swapaxes(block[:s], 0, 1), jnp.swapaxes(block[s:], 0, 1)
        both = jnp.concatenate(exchange_halves(low, high, left), axis=1)
        return both.astype(bf16)

    back = []
    for k in range(1, rows):
        to = lax.rem(row + k, rows)
        send_v[k - 1] = block_back(to)
        copy = remote(send_v.at[k - 1], got_v.at[row], back_sem, k - 1, (to, col))
        copy.start()
        back.append(copy)
    got_v[row] = block_back(row)
    pack_grads(vert[...].reshape(ny * nu * sv, LANES), stacked, r_v, payload, 1)
    sum_v.scatter()
    clear_dpre(d_h, r_h, nx, 2 * REACH, gh)
    for u in range(nu):
        for m in range(ny // 2):
            here = (u * ny // 2 + m) * LANES
            one, two = exchange_halves(vout[2 * m, u], vout[2 * m + 1, u], left2)
            o_ref[0, :, here : here + LANES] = one.astype(bf16)
            o_ref[1, :, here : here + LANES] = two.astype(bf16)
    for copy in back:
        copy.wait_recv()
    for r in range(rows):
        grad_h[:, r * 2 * s : (r + 1) * 2 * s] = got_v[r].astype(f32)

    def third_pass(x, carry):
        grad = grad_h[x].reshape(shape_h)
        for index, shift in enumerate(SHIFTS):
            place = place_of(x, shift, nv, shape_h, start)
            p = pre_ref[index, x]
            keep = (place >= 0) & (place < x_all)
            blend = b_ref[0, index : index + 1]
            store_dpre(
                d_h, r_h, x + 2 * REACH, index, gh, keep, grad, blend, p, sigma_of(p)
            )
        return carry

    lax.fori_loop(0, nx, third_pass, 0)
    sum_v.exchange()
    gather_dpre(d_h, s_ref, nx + 2 * REACH, nv, gh, start - REACH, x_all)
    stacked = s_ref[: (nx + 2 * REACH) * nvs]
    pack_grads(wide[...].reshape((nx + 2 * REACH) * nvs, LANES), stacked, r_h, payload, 0)
    sum_h.scatter()
    sum_v.gather()
    grads = jnp.dot(stacked, w_ref[0], preferred_element_type=f32)
    grads = grads.reshape(nx + 2 * REACH, nvs, LANES)
    rim_sent[0] = grads[:REACH].astype(bf16)
    rim_sent[1] = grads[nx + REACH :].astype(bf16)
    rims = [
        remote(rim_sent.at[0], rim_got.at[1], rim_sem, 0, (row, left_col)),
        remote(rim_sent.at[1], rim_got.at[0], rim_sem, 1, (row, right_col)),
    ]
    for copy in rims:
        copy.start()
    grad_h[...] += grads[REACH : REACH + nx]
    sum_h.exchange()
    for copy in rims:
        copy.wait_recv()

    @pl.when(col > 0)
    def _():
        grad_h[:REACH] += rim_got[0].astype(f32)

    @pl.when(col < cols - 1)
    def _():
        grad_h[nx - REACH :] += rim_got[1].astype(f32)

    sum_h.gather()
    for m in range(nv // 2):
        one = grad_h[:, 2 * m * s : (2 * m + 1) * s]
        two = grad_h[:, (2 * m + 1) * s : (2 * m + 2) * s]
        low, high = exchange_halves(one, two, left)
        lanes = slice(m * LANES, (m + 1) * LANES)
        dhor_ref[:s, :, lanes] = jnp.swapaxes(low, 0, 1).astype(bf16)
        dhor_ref[s:, :, lanes] = jnp.swapaxes(high, 0, 1).astype(bf16)
    factor = float(nu * ny * nv * x_all) ** (-0.5)
    sum_v.finish()
    unpack_grads(sum_ref, 1, shear_ref, gw_v_ref, gb_v_ref, factor)
    sum_h.finish()
    unpack_grads(sum_ref, 0, shear_ref, gw_h_ref, gb_h_ref, factor)
    for copy in halo + there + back + rims:
        copy.wait_send()


def per_device(features, weight_h, weight_v, beta_h, beta_v, shear_set, cotangent):
    rows, cols = lax.axis_size("vrow"), lax.axis_size("img")
    channels = weight_h.shape[0]
    u_local, y_all, x_local, merged = features.shape
    v_all = merged // channels
    v_local = v_all // rows
    u_all = u_local * rows
    s_h = u_local * y_all // 2
    s_v = v_local * x_local // 2
    f32, bf16 = jnp.float32, jnp.bfloat16
    count = len(SHIFTS)
    assert u_local == 1 and v_local == 2 and s_h % 8 == 0 and s_v % 8 == 0

    def tap_major(weight):
        return jnp.transpose(weight, (2, 3, 0, 1)).reshape(9, channels, channels)

    flat_h = (x_local, v_all * s_h, LANES)
    flat_v = (y_all, u_all * s_v, LANES)
    four_v = (y_all, u_all, s_v, LANES)
    rim = (REACH, v_all * s_h, LANES)
    grads = 5 * channels
    chunk = (grads // cols, LANES)
    gh, gv = s_h // 8, s_v // 8
    wide_x, wide_y = x_local + 2 * REACH, y_all + 2 * REACH
    products = max(wide_x * (v_all + 2) * gh, wide_y * (u_all + 2) * gv)
    vmem, dma = pltpu.VMEM, pltpu.SemaphoreType.DMA
    whole = pl.BlockSpec(memory_space=vmem)
    shape = jax.ShapeDtypeStruct
    output, dhor, gw_h, gw_v, gb_h, gb_v = pl.pallas_call(
        functools.partial(field_kernel, rows, cols),
        out_shape=[
            shape(cotangent.shape, bf16),
            shape(features.shape[1:], bf16),
            shape((9, channels, channels), f32),
            shape((9, channels, channels), f32),
            shape(beta_h.shape, f32),
            shape(beta_v.shape, f32),
        ],
        in_specs=[whole] * 5 + [pl.BlockSpec(memory_space=pltpu.SMEM), whole],
        out_specs=[whole] * 6,
        scratch_shapes=[
            vmem((wide_x,) + flat_h[1:], bf16),
            vmem((2, 9 * LANES, LANES), bf16),
            vmem((2, 8, LANES), f32),
            vmem((9, products, 8, LANES), f32),
            vmem((count, x_local, v_all * gh, 8, LANES), f32),
            vmem((x_local, v_all, s_h, LANES), f32),
            vmem((rows - 1, y_all * s_v, LANES), bf16),
            vmem((rows, y_all * s_v, LANES), bf16),
            vmem(flat_v, bf16),
            vmem(four_v, f32),
            vmem(four_v, f32),
            vmem(four_v, f32),
            vmem((rows - 1, x_local, 2 * s_h, LANES), bf16),
            vmem((rows, x_local, 2 * s_h, LANES), bf16),
            vmem(flat_h, f32),
            vmem((2,) + rim, bf16),
            vmem((2,) + rim, bf16),
            vmem((2, grads, LANES), f32),
            vmem((2, grads, LANES), f32),
            vmem((2, cols - 1) + chunk, f32),
            vmem((2, rows) + chunk, f32),
            vmem((max(wide_x * flat_h[1], y_all * flat_v[1]), 9 * LANES), bf16),
            vmem((count, x_local + 4 * REACH, (v_all + 2) * gh, 8, LANES), f32),
            vmem((count, wide_y, (u_all + 2) * gv, 8, LANES), f32),
            vmem((count, 8, LANES), f32),
            vmem((count, 8, LANES), f32),
            dma((2, 2)),
            dma((2, rows - 1)),
            dma((2, rows - 1)),
            dma((2, 2)),
            dma((2, 2, cols - 1)),
            dma((2, 2, rows - 1)),
            dma((2, 2, cols - 1)),
        ],
        compiler_params=pltpu.CompilerParams(
            collective_id=0, has_side_effects=True, vmem_limit_bytes=VMEM_LIMIT
        ),
        name="light_field",
    )(
        features.reshape(features.shape[1:]),
        tap_major(weight_h),
        tap_major(weight_v),
        beta_h,
        beta_v,
        shear_set,
        cotangent,
    )

    def tap_minor(grad):
        return jnp.transpose(grad.reshape(3, 3, channels, channels), (2, 3, 0, 1))

    return output, dhor.reshape(features.shape), tap_minor(gw_h), tap_minor(gw_v), gb_h, gb_v


def solution(mesh):
    placed = (P("vrow", None, "img", None), P(), P(), P(), P(), P(), P("vrow", "img", None))
    return jax.shard_map(
        per_device,
        mesh=mesh,
        in_specs=placed,
        out_specs=(P("vrow", "img", None), P("vrow", None, "img", None), P(), P(), P(), P()),
        check_vma=False,
    )
```

time: 56.8 us -> 47 us (0.83)
  other arithmetic: 4.58 us -> 0 us
  local copies, waits for them, and re-layouts: 10.3 us -> 6.23 us
  Pallas kernels: 40.5 us -> 39.5 us
    unnamed x10 -> x14, local copies, waits for them, and re-layouts: 0.62 us -> 6.23 us
    reshape x10 -> x0, local copies, waits for them, and re-layouts: 4.66 us -> none  [the longest x1 0.93 us: per_device(): output = output.reshape(v_local, x_local, u_all * y_all * channels)]
    mul x6 -> x0, local copies, waits for them, and re-layouts: 2.8 us -> none  [the longest x4 2.04 us: per_device(): weights[:, None, :, :, None, :] * eye[None, :, None, None, :, None]]
    mul x2 -> x0, other arithmetic: 1.88 us -> none  [the longest x1 1 us: per_device(): summed = summed * factor]
    transpose x1 -> x0, other arithmetic: 1.04 us -> none  [per_device(): weights = jnp.transpose(weights, (0, 2, 3, 1))]
    pallas_call x1, Pallas kernels: 40.5 us -> 39.5 us  [per_device(): pl.pallas_call(functools.partial(field_kernel, rows, cols), out_shape=[sh...]
    slice x3 -> x0, local copies, waits for them, and re-layouts: 0.86 us -> none  [the longest x2 0.86 us: per_device(): return (output, dhor, by_tap[0], by_tap[1], grad_beta[0], grad_beta[1])]
    convert_element_type x2 -> x0, other arithmetic: 0.75 us -> none  [the longest x1 0.75 us: per_device(): (jnp.asarray(SHIFTS, jnp.int32)[:, None] == shear_set[None, :]).astype(f32)]
where the time goes in v2:
time: 47 us; the launch traced here: 46.4 us
  Pallas kernels  39.5 us (84%)
  local copies, waits for them, and re-layouts  6.23 us (13%)
  between operations  0.66 us (1%)
    pallas_call x1, Pallas kernels, per_device(): pl.pallas_call(functools.partial(field_kernel, rows, cols), out_shape=[sh...  39.5 us
    unnamed x14, local copies, waits for them, and re-layouts  6.23 us

profile of v2, /device:TPU:1, one launch (start us, length us, event | category | flops | bytes accessed | tf_op | source)
XLA Modules:
  0.0 46.4 jit_solution(7614476140638828407)
XLA Ops:
  0.6 39.5 %light_field.1 = (bf16[2,8,4096]{2,1,0:T(8,128)(2,1)}, bf16[16,8,512]{2,1,0:T(8,128)(2,1)}, f32[9,64,64]{2,1,0:T(8,128)}, f32[9,64,64]{2,1,0:T(8,128)}, f32[5,64]{1,0:T(8,128)}, /*index=5*/f32[5,64]{1,0:T(8,128)}) custom-call(bf16[16,8,512]{2,1,0:T(8,128)(2,1)} %bitcast.18, bf16[9,64,64]{2,1,0:T(8,128)(2,1)} %bitcast.16, bf16[9,64,64]{2,1,0:T(8,128)(2,1)} %bitcast.17, ...), custom_call_target="tpu_custom_call" | custom-call | tf_op jit(solution)/shard_map/light_field/pallas_call | solution.py:574
  40.1 0.0 copy-start.1
  40.1 1.6 %copy.19 = bf16[2,8,4096]{2,1,0:T(8,128)(2,1)} copy(bf16[2,8,4096]{2,1,0:T(8,128)(2,1)} %get-tuple-element.24) | data formatting | bytes 262144
  41.8 1.6 %copy.20 = bf16[1,16,8,512]{3,2,1,0:T(8,128)(2,1)} copy(bf16[1,16,8,512]{3,2,1,0:T(8,128)(2,1)} %bitcast.19) | data formatting | bytes 262144
  43.3 0.0 copy-done.1
  43.3 0.0 copy-start
  43.3 0.7 %copy.21 = f32[64,64,3,3]{1,0,3,2:T(8,128)} copy(f32[64,64,3,3]{1,0,3,2:T(8,128)S(1)} %bitcast.15) | data formatting | bytes 294912
  44.0 0.4 copy-done
  44.4 0.0 copy-start.3
  44.4 0.7 %copy.22 = f32[64,64,3,3]{1,0,3,2:T(8,128)} copy(f32[64,64,3,3]{1,0,3,2:T(8,128)S(1)} %bitcast.14) | data formatting | bytes 294912
  45.1 0.0 copy-done.3
  45.1 0.0 copy-start.2
  45.1 0.6 %copy.23 = f32[5,64]{1,0:T(8,128)} copy(f32[5,64]{1,0:T(8,128)S(1)} %copy-done.3) | data formatting | bytes 2560
  45.7 0.1 copy-done.2
  45.8 0.6 %copy.24 = f32[5,64]{1,0:T(8,128)} copy(f32[5,64]{1,0:T(8,128)S(1)} %copy-done.2) | data formatting | bytes 2560
Async XLA Ops:
  40.1 3.2 %copy-start.1 = (f32[9,64,64]{2,1,0:T(8,128)S(1)}, f32[9,64,64]{2,1,0:T(8,128)}, u32[]{:S(2)}) copy-start(f32[9,64,64]{2,1,0:T(8,128)} %get-tuple-element.14) | copy-start | bytes 442372
  43.3 1.1 %copy-start = (f32[9,64,64]{2,1,0:T(8,128)S(1)}, f32[9,64,64]{2,1,0:T(8,128)}, u32[]{:S(2)}) copy-start(f32[9,64,64]{2,1,0:T(8,128)} %get-tuple-element.15) | copy-start | bytes 442372
  44.4 0.7 %copy-start.3 = (f32[5,64]{1,0:T(8,128)S(1)}, f32[5,64]{1,0:T(8,128)}, u32[]{:S(2)}) copy-start(f32[5,64]{1,0:T(8,128)} %get-tuple-element.28) | copy-start | bytes 3844
  45.1 0.7 %copy-start.2 = (f32[5,64]{1,0:T(8,128)S(1)}, f32[5,64]{1,0:T(8,128)}, u32[]{:S(2)}) copy-start(f32[5,64]{1,0:T(8,128)} %get-tuple-element.29) | copy-start | bytes 3844

commit v3 on v2

--- a/solution.py
+++ b/solution.py
@@ -15,8 +15,9 @@
 VMEM_LIMIT = 60 * 1024 * 1024
 
 
-def place_of(x, shift, views, shape, start):
-    view = lax.broadcasted_iota(jnp.int32, shape, 0) // (shape[0] // views) - views // 2
+def place_of(x, shift, views, shape, start, middle=None):
+    middle = views // 2 if middle is None else middle
+    view = lax.broadcasted_iota(jnp.int32, shape, 0) // (shape[0] // views) - middle
     return start + x - shift * view
 
 
@@ -57,12 +58,13 @@
         z_ref[:, (columns - rim) * step : columns * step] = zero
 
 
-def preact_at(z_ref, x, views, group, shift, place, total):
+def preact_at(z_ref, x, views, group, shift, place, total, first=0, width=None):
+    per = (views if width is None else width) * group
     step = (views + 2) * group
     sums = {}
     for t, (i, j) in enumerate(TAPS):
-        here = (x + (REACH + j + shift * i)) * step + (1 + i) * group
-        term = z_ref[t, pl.ds(here, views * group)]
+        here = (x + (REACH + j + shift * i)) * step + (1 + i + first) * group
+        term = z_ref[t, pl.ds(here, per)]
         sums[j] = term if j not in sums else sums[j] + term
     low = jnp.where(place != 0, sums[-1], 0.0)
     high = jnp.where(place != total - 1, sums[1], 0.0)
@@ -368,33 +370,40 @@
     tap_products(wide, w_ref, 0, z_ref, nv, 0, REACH)
     tap_products(wide, w_ref, 0, z_ref, nv, nx + REACH, REACH)
 
-    def first_pass(x, carry):
-        out = wide[x + REACH].astype(f32).reshape(shape_h)
-        for index, shift in enumerate(SHIFTS):
-            place = place_of(x, shift, nv, shape_h, start)
-            p = preact_at(z_ref, x, nv, gh, shift, place, x_all)
-            pre_ref[index, x] = p
-            keep = (place >= 0) & (place < x_all)
-            out = out + b_ref[0, index : index + 1] * jnp.where(keep, p * sigma_of(p), 0.0)
-        hfeat[x] = out.reshape(nv, s, LANES)
-        return carry
-
-    lax.fori_loop(0, nx, first_pass, 0)
-
-    def block_there(to):
-        views = hfeat[:, pl.ds(2 * to, 2)]
-        low, high = exchange_halves(views[:, 0], views[:, 1], left)
+    shape_two = (2 * gh, 8, LANES)
+    unroll = 4 if nx % 4 == 0 else 1
+
+    def first_pass(to):
+        rows_two = pl.ds(pl.multiple_of(to * (2 * s), 16), 2 * s)
+
+        def column(x):
+            out = wide[x + REACH, rows_two].astype(f32).reshape(shape_two)
+            for index, shift in enumerate(SHIFTS):
+                place = place_of(x, shift, 2, shape_two, start, nv // 2 - 2 * to)
+                p = preact_at(z_ref, x, nv, gh, shift, place, x_all, 2 * to, 2)
+                pre_ref[index, x, pl.ds(2 * to * gh, 2 * gh)] = p
+                keep = (place >= 0) & (place < x_all)
+                out = out + b_ref[0, index : index + 1] * jnp.where(keep, p * sigma_of(p), 0.0)
+            hfeat[x] = out.reshape(2, s, LANES)
+
+        def body(step, carry):
+            for k in range(unroll):
+                column(step * unroll + k)
+            return carry
+
+        lax.fori_loop(0, nx // unroll, body, 0)
+        low, high = exchange_halves(hfeat[:, 0], hfeat[:, 1], left)
         both = [jnp.swapaxes(low, 0, 1), jnp.swapaxes(high, 0, 1)]
         return jnp.concatenate(both, axis=0).reshape(ny * sv, LANES).astype(bf16)
 
     there = []
     for k in range(1, rows):
         to = lax.rem(row + k, rows)
-        send_h[k - 1] = block_there(to)
+        send_h[k - 1] = first_pass(to)
         copy = remote(send_h.at[k - 1], got_h.at[row], there_sem, k - 1, (to, col))
         copy.start()
         there.append(copy)
-    got_h[row] = block_there(row)
+    got_h[row] = first_pass(row)
 
     sum_h, sum_v = [
         Sum(
@@ -483,6 +492,7 @@
         copy.wait_recv()
     for r in range(rows):
         grad_h[:, r * 2 * s : (r + 1) * 2 * s] = got_v[r].astype(f32)
+    sum_v.exchange()
 
     def third_pass(x, carry):
         grad = grad_h[x].reshape(shape_h)
@@ -497,12 +507,11 @@
         return carry
 
     lax.fori_loop(0, nx, third_pass, 0)
-    sum_v.exchange()
+    sum_v.gather()
     gather_dpre(d_h, s_ref, nx + 2 * REACH, nv, gh, start - REACH, x_all)
     stacked = s_ref[: (nx + 2 * REACH) * nvs]
     pack_grads(wide[...].reshape((nx + 2 * REACH) * nvs, LANES), stacked, r_h, payload, 0)
     sum_h.scatter()
-    sum_v.gather()
     grads = jnp.dot(stacked, w_ref[0], preferred_element_type=f32)
     grads = grads.reshape(nx + 2 * REACH, nvs, LANES)
     rim_sent[0] = grads[:REACH].astype(bf16)
@@ -515,6 +524,9 @@
         copy.start()
     grad_h[...] += grads[REACH : REACH + nx]
     sum_h.exchange()
+    factor = float(nu * ny * nv * x_all) ** (-0.5)
+    sum_v.finish()
+    unpack_grads(sum_ref, 1, shear_ref, gw_v_ref, gb_v_ref, factor)
     for copy in rims:
         copy.wait_recv()
 
@@ -534,13 +546,34 @@
         lanes = slice(m * LANES, (m + 1) * LANES)
         dhor_ref[:s, :, lanes] = jnp.swapaxes(low, 0, 1).astype(bf16)
         dhor_ref[s:, :, lanes] = jnp.swapaxes(high, 0, 1).astype(bf16)
-    factor = float(nu * ny * nv * x_all) ** (-0.5)
-    sum_v.finish()
-    unpack_grads(sum_ref, 1, shear_ref, gw_v_ref, gb_v_ref, factor)
     sum_h.finish()
     unpack_grads(sum_ref, 0, shear_ref, gw_h_ref, gb_h_ref, factor)
     for copy in halo + there + back + rims:
         copy.wait_send()
+
+
+def hand_out_kernel(*refs):
+    count = len(refs) // 2
+    copies = [
+        pltpu.make_async_copy(refs[k], refs[count + k], refs[-1].at[k]) for k in range(count)
+    ]
+    for copy in copies:
+        copy.start()
+    for copy in copies:
+        copy.wait()
+
+
+def hand_out(*arrays):
+    anywhere = pl.BlockSpec(memory_space=pl.ANY)
+    return pl.pallas_call(
+        hand_out_kernel,
+        out_shape=[jax.ShapeDtypeStruct(a.shape, a.dtype) for a in arrays],
+        in_specs=[anywhere] * len(arrays),
+        out_specs=[anywhere] * len(arrays),
+        scratch_shapes=[pltpu.SemaphoreType.DMA((len(arrays),))],
+        compiler_params=pltpu.CompilerParams(vmem_limit_bytes=VMEM_LIMIT),
+        name="hand_out",
+    )(*arrays)
 
 
 def per_device(features, weight_h, weight_v, beta_h, beta_v, shear_set, cotangent):
@@ -571,7 +604,7 @@
     vmem, dma = pltpu.VMEM, pltpu.SemaphoreType.DMA
     whole = pl.BlockSpec(memory_space=vmem)
     shape = jax.ShapeDtypeStruct
-    output, dhor, gw_h, gw_v, gb_h, gb_v = pl.pallas_call(
+    results = pl.pallas_call(
         functools.partial(field_kernel, rows, cols),
         out_shape=[
             shape(cotangent.shape, bf16),
@@ -589,7 +622,7 @@
             vmem((2, 8, LANES), f32),
             vmem((9, products, 8, LANES), f32),
             vmem((count, x_local, v_all * gh, 8, LANES), f32),
-            vmem((x_local, v_all, s_h, LANES), f32),
+            vmem((x_local, 2, s_h, LANES), f32),
             vmem((rows - 1, y_all * s_v, LANES), bf16),
             vmem((rows, y_all * s_v, LANES), bf16),
             vmem(flat_v, bf16),
@@ -632,6 +665,8 @@
         cotangent,
     )
 
+    output, dhor, gw_h, gw_v, gb_h, gb_v = hand_out(*results)
+
     def tap_minor(grad):
         return jnp.transpose(grad.reshape(3, 3, channels, channels), (2, 3, 0, 1))
 

time: 47 us -> 69.8 us (1.49)
  Pallas kernels: 39.5 us -> 68.6 us
  local copies, waits for them, and re-layouts: 6.23 us -> 0 us
    pallas_call x0 -> x1, Pallas kernels: none -> 27.1 us  [hand_out(): pl.pallas_call(hand_out_kernel, out_shape=[jax.ShapeDtypeStruct(a.shape,...]
    unnamed x14 -> x0, local copies, waits for them, and re-layouts: 6.23 us -> none
    pallas_call x1, Pallas kernels: 39.5 us -> 41.5 us  [per_device(): pl.pallas_call(functools.partial(field_kernel, rows, cols), out_shape=[sh...]
where the time goes in v3:
time: 69.8 us; the launch traced here: 69.3 us
  Pallas kernels  68.6 us (98%)
    pallas_call x1, Pallas kernels, per_device(): pl.pallas_call(functools.partial(field_kernel, rows, cols), out_shape=[sh...  41.5 us
    pallas_call x1, Pallas kernels, hand_out(): pl.pallas_call(hand_out_kernel, out_shape=[jax.ShapeDtypeStruct(a.shape,...  27.1 us

profile of v3, /device:TPU:1, one launch (start us, length us, event | category | flops | bytes accessed | tf_op | source)
XLA Modules:
  0.0 69.3 jit_solution(14101076821544774131)
XLA Ops:
  0.6 41.5 %light_field.1 = (bf16[2,8,4096]{2,1,0:T(8,128)(2,1)}, bf16[16,8,512]{2,1,0:T(8,128)(2,1)}, f32[9,64,64]{2,1,0:T(8,128)}, f32[9,64,64]{2,1,0:T(8,128)}, f32[5,64]{1,0:T(8,128)}, /*index=5*/f32[5,64]{1,0:T(8,128)}) custom-call(bf16[16,8,512]{2,1,0:T(8,128)(2,1)} %bitcast.16, bf16[9,64,64]{2,1,0:T(8,128)(2,1)} %bitcast.14, bf16[9,64,64]{2,1,0:T(8,128)(2,1)} %bitcast.15, ...), custom_call_target="tpu_custom_call" | custom-call | tf_op jit(solution)/shard_map/light_field/pallas_call | solution.py:607
  42.2 27.1 %hand_out.1 = (bf16[2,8,4096]{2,1,0:T(8,128)(2,1)}, bf16[16,8,512]{2,1,0:T(8,128)(2,1)}, f32[9,64,64]{2,1,0:T(8,128)}, f32[9,64,64]{2,1,0:T(8,128)}, f32[5,64]{1,0:T(8,128)}, /*index=5*/f32[5,64]{1,0:T(8,128)}) custom-call(bf16[2,8,4096]{2,1,0:T(8,128)(2,1)} %get-tuple-element.18.refs_0_, bf16[16,8,512]{2,1,0:T(8,128)(2,1)} %get-tuple-element.19.refs_1_, ...), custom_call_target="tpu_custom_call" | custom-call | tf_op jit(solution)/shard_map/hand_out/pallas_call | solution.py:568

commit v4 on v2

--- a/solution.py
+++ b/solution.py
@@ -483,6 +483,7 @@
         copy.wait_recv()
     for r in range(rows):
         grad_h[:, r * 2 * s : (r + 1) * 2 * s] = got_v[r].astype(f32)
+    sum_v.exchange()
 
     def third_pass(x, carry):
         grad = grad_h[x].reshape(shape_h)
@@ -497,12 +498,11 @@
         return carry
 
     lax.fori_loop(0, nx, third_pass, 0)
-    sum_v.exchange()
+    sum_v.gather()
     gather_dpre(d_h, s_ref, nx + 2 * REACH, nv, gh, start - REACH, x_all)
     stacked = s_ref[: (nx + 2 * REACH) * nvs]
     pack_grads(wide[...].reshape((nx + 2 * REACH) * nvs, LANES), stacked, r_h, payload, 0)
     sum_h.scatter()
-    sum_v.gather()
     grads = jnp.dot(stacked, w_ref[0], preferred_element_type=f32)
     grads = grads.reshape(nx + 2 * REACH, nvs, LANES)
     rim_sent[0] = grads[:REACH].astype(bf16)
@@ -515,6 +515,9 @@
         copy.start()
     grad_h[...] += grads[REACH : REACH + nx]
     sum_h.exchange()
+    factor = float(nu * ny * nv * x_all) ** (-0.5)
+    sum_v.finish()
+    unpack_grads(sum_ref, 1, shear_ref, gw_v_ref, gb_v_ref, factor)
     for copy in rims:
         copy.wait_recv()
 
@@ -534,13 +537,28 @@
         lanes = slice(m * LANES, (m + 1) * LANES)
         dhor_ref[:s, :, lanes] = jnp.swapaxes(low, 0, 1).astype(bf16)
         dhor_ref[s:, :, lanes] = jnp.swapaxes(high, 0, 1).astype(bf16)
-    factor = float(nu * ny * nv * x_all) ** (-0.5)
-    sum_v.finish()
-    unpack_grads(sum_ref, 1, shear_ref, gw_v_ref, gb_v_ref, factor)
     sum_h.finish()
     unpack_grads(sum_ref, 0, shear_ref, gw_h_ref, gb_h_ref, factor)
     for copy in halo + there + back + rims:
         copy.wait_send()
+
+
+def hand_out_kernel(*refs):
+    count = len(refs) // 2
+    for source, target in zip(refs[:count], refs[count:]):
+        target[...] = source[...]
+
+
+def hand_out(*arrays):
+    whole = pl.BlockSpec(memory_space=pltpu.VMEM)
+    return pl.pallas_call(
+        hand_out_kernel,
+        out_shape=[jax.ShapeDtypeStruct(a.shape, a.dtype) for a in arrays],
+        in_specs=[whole] * len(arrays),
+        out_specs=[whole] * len(arrays),
+        compiler_params=pltpu.CompilerParams(vmem_limit_bytes=VMEM_LIMIT),
+        name="hand_out",
+    )(*arrays)
 
 
 def per_device(features, weight_h, weight_v, beta_h, beta_v, shear_set, cotangent):
@@ -571,7 +589,7 @@
     vmem, dma = pltpu.VMEM, pltpu.SemaphoreType.DMA
     whole = pl.BlockSpec(memory_space=vmem)
     shape = jax.ShapeDtypeStruct
-    output, dhor, gw_h, gw_v, gb_h, gb_v = pl.pallas_call(
+    results = pl.pallas_call(
         functools.partial(field_kernel, rows, cols),
         out_shape=[
             shape(cotangent.shape, bf16),
@@ -632,6 +650,8 @@
         cotangent,
     )
 
+    output, dhor, gw_h, gw_v, gb_h, gb_v = hand_out(*results)
+
     def tap_minor(grad):
         return jnp.transpose(grad.reshape(3, 3, channels, channels), (2, 3, 0, 1))
 

time: 47 us -> 45.3 us (0.964)
  local copies, waits for them, and re-layouts: 6.23 us -> 0 us
  Pallas kernels: 39.5 us -> 44.1 us
    unnamed x14 -> x0, local copies, waits for them, and re-layouts: 6.23 us -> none
    pallas_call x1, Pallas kernels: 39.5 us -> 42 us  [per_device(): pl.pallas_call(functools.partial(field_kernel, rows, cols), out_shape=[sh...]
    pallas_call x0 -> x1, Pallas kernels: none -> 2.1 us  [hand_out(): pl.pallas_call(hand_out_kernel, out_shape=[jax.ShapeDtypeStruct(a.shape,...]
where the time goes in v4:
time: 45.3 us; the launch traced here: 44.8 us
  Pallas kernels  44.1 us (97%)
  between operations  0.64 us (1%)
    pallas_call x1, Pallas kernels, per_device(): pl.pallas_call(functools.partial(field_kernel, rows, cols), out_shape=[sh...  42 us
    pallas_call x1, Pallas kernels, hand_out(): pl.pallas_call(hand_out_kernel, out_shape=[jax.ShapeDtypeStruct(a.shape,...  2.1 us

profile of v4, /device:TPU:1, one launch (start us, length us, event | category | flops | bytes accessed | tf_op | source)
XLA Modules:
  0.0 44.8 jit_solution(14734128405106915888)
XLA Ops:
  0.6 42.0 %light_field.1 = (bf16[2,8,4096]{2,1,0:T(8,128)(2,1)}, bf16[16,8,512]{2,1,0:T(8,128)(2,1)}, f32[9,64,64]{2,1,0:T(8,128)}, f32[9,64,64]{2,1,0:T(8,128)}, f32[5,64]{1,0:T(8,128)}, /*index=5*/f32[5,64]{1,0:T(8,128)}) custom-call(bf16[16,8,512]{2,1,0:T(8,128)(2,1)} %bitcast.16, bf16[9,64,64]{2,1,0:T(8,128)(2,1)} %bitcast.14, bf16[9,64,64]{2,1,0:T(8,128)(2,1)} %bitcast.15, ...), custom_call_target="tpu_custom_call" | custom-call | tf_op jit(solution)/shard_map/light_field/pallas_call | solution.py:592
  42.7 2.1 %hand_out.1 = (bf16[2,8,4096]{2,1,0:T(8,128)(2,1)}, bf16[16,8,512]{2,1,0:T(8,128)(2,1)}, f32[9,64,64]{2,1,0:T(8,128)}, f32[9,64,64]{2,1,0:T(8,128)}, f32[5,64]{1,0:T(8,128)}, /*index=5*/f32[5,64]{1,0:T(8,128)}) custom-call(bf16[2,8,4096]{2,1,0:T(8,128)(2,1)} %get-tuple-element.18.refs_0_, bf16[16,8,512]{2,1,0:T(8,128)(2,1)} %get-tuple-element.19.refs_1_, ...), custom_call_target="tpu_custom_call" | custom-call | tf_op jit(solution)/shard_map/hand_out/pallas_call | solution.py:554

commit v5 on v4

--- a/solution.py
+++ b/solution.py
@@ -483,7 +483,6 @@
         copy.wait_recv()
     for r in range(rows):
         grad_h[:, r * 2 * s : (r + 1) * 2 * s] = got_v[r].astype(f32)
-    sum_v.exchange()
 
     def third_pass(x, carry):
         grad = grad_h[x].reshape(shape_h)
@@ -498,11 +497,12 @@
         return carry
 
     lax.fori_loop(0, nx, third_pass, 0)
-    sum_v.gather()
+    sum_v.exchange()
     gather_dpre(d_h, s_ref, nx + 2 * REACH, nv, gh, start - REACH, x_all)
     stacked = s_ref[: (nx + 2 * REACH) * nvs]
     pack_grads(wide[...].reshape((nx + 2 * REACH) * nvs, LANES), stacked, r_h, payload, 0)
     sum_h.scatter()
+    sum_v.gather()
     grads = jnp.dot(stacked, w_ref[0], preferred_element_type=f32)
     grads = grads.reshape(nx + 2 * REACH, nvs, LANES)
     rim_sent[0] = grads[:REACH].astype(bf16)
@@ -515,9 +515,6 @@
         copy.start()
     grad_h[...] += grads[REACH : REACH + nx]
     sum_h.exchange()
-    factor = float(nu * ny * nv * x_all) ** (-0.5)
-    sum_v.finish()
-    unpack_grads(sum_ref, 1, shear_ref, gw_v_ref, gb_v_ref, factor)
     for copy in rims:
         copy.wait_recv()
 
@@ -537,6 +534,9 @@
         lanes = slice(m * LANES, (m + 1) * LANES)
         dhor_ref[:s, :, lanes] = jnp.swapaxes(low, 0, 1).astype(bf16)
         dhor_ref[s:, :, lanes] = jnp.swapaxes(high, 0, 1).astype(bf16)
+    factor = float(nu * ny * nv * x_all) ** (-0.5)
+    sum_v.finish()
+    unpack_grads(sum_ref, 1, shear_ref, gw_v_ref, gb_v_ref, factor)
     sum_h.finish()
     unpack_grads(sum_ref, 0, shear_ref, gw_h_ref, gb_h_ref, factor)
     for copy in halo + there + back + rims:

time: 45.3 us -> 42.7 us (0.943)
  Pallas kernels: 44.1 us -> 41.6 us
    pallas_call x1, Pallas kernels: 42 us -> 39.5 us  [per_device(): pl.pallas_call(functools.partial(field_kernel, rows, cols), out_shape=[sh...]
where the time goes in v5:
time: 42.7 us; the launch traced here: 42.2 us
  Pallas kernels  41.6 us (97%)
  between operations  0.64 us (1%)
    pallas_call x1, Pallas kernels, per_device(): pl.pallas_call(functools.partial(field_kernel, rows, cols), out_shape=[sh...  39.5 us
    pallas_call x1, Pallas kernels, hand_out(): pl.pallas_call(hand_out_kernel, out_shape=[jax.ShapeDtypeStruct(a.shape,...  2.1 us

profile of v5, /device:TPU:1, one launch (start us, length us, event | category | flops | bytes accessed | tf_op | source)
XLA Modules:
  0.0 42.2 jit_solution(9467151095346746779)
XLA Ops:
  0.6 39.5 %light_field.1 = (bf16[2,8,4096]{2,1,0:T(8,128)(2,1)}, bf16[16,8,512]{2,1,0:T(8,128)(2,1)}, f32[9,64,64]{2,1,0:T(8,128)}, f32[9,64,64]{2,1,0:T(8,128)}, f32[5,64]{1,0:T(8,128)}, /*index=5*/f32[5,64]{1,0:T(8,128)}) custom-call(bf16[16,8,512]{2,1,0:T(8,128)(2,1)} %bitcast.16, bf16[9,64,64]{2,1,0:T(8,128)(2,1)} %bitcast.14, bf16[9,64,64]{2,1,0:T(8,128)(2,1)} %bitcast.15, ...), custom_call_target="tpu_custom_call" | custom-call | tf_op jit(solution)/shard_map/light_field/pallas_call | solution.py:592
  40.1 2.1 %hand_out.1 = (bf16[2,8,4096]{2,1,0:T(8,128)(2,1)}, bf16[16,8,512]{2,1,0:T(8,128)(2,1)}, f32[9,64,64]{2,1,0:T(8,128)}, f32[9,64,64]{2,1,0:T(8,128)}, f32[5,64]{1,0:T(8,128)}, /*index=5*/f32[5,64]{1,0:T(8,128)}) custom-call(bf16[2,8,4096]{2,1,0:T(8,128)(2,1)} %get-tuple-element.18.refs_0_, bf16[16,8,512]{2,1,0:T(8,128)(2,1)} %get-tuple-element.19.refs_1_, ...), custom_call_target="tpu_custom_call" | custom-call | tf_op jit(solution)/shard_map/hand_out/pallas_call | solution.py:554
